TPU v7x, 32 devices: a whole 2x2x4 slice. The times are simulated.
32 devices in a mesh: tm: 8 (over z, y), chan: 4 (over x, core).
Axes of the slice: x: 2, y: 2, z: 4, core: 2. Of those that a mesh axis runs over, the one named last changes fastest.
Arguments:
- spectrogram_input: bfloat16 [512, 8192], P('chan', 'tm'), may hold values from -6 to 6
- upsample_direction: float32 [16, 256, 512], P(None, 'chan'), may hold values from -0.09375 to 0.09375
- upsample_magnitude: float32 [512], replicated, may hold values from 0.5 to 2
- upsample_bias: float32 [256], P('chan'), may hold values from -3 to 3
- dilated_direction: float32 [3, 3, 256, 256], P(None, None, 'chan'), may hold values from -0.21875 to 0.21875
- dilated_magnitude: float32 [3, 256], P(None, 'chan'), may hold values from 0.5 to 2
- dilated_bias: float32 [3, 256], P(None, 'chan'), may hold values from -3 to 3
- pointwise_direction: float32 [3, 256, 256], P(None, 'chan'), may hold values from -0.375 to 0.375
- pointwise_magnitude: float32 [3, 256], P(None, 'chan'), may hold values from 0.5 to 2
- block_output_bias: float32 [3, 256], P(None, 'chan'), may hold values from -3 to 3
- shortcut_direction: float32 [3, 256, 256], P(None, 'chan'), may hold values from -0.375 to 0.375
- shortcut_magnitude: float32 [3, 256], P(None, 'chan'), may hold values from 0.5 to 2
- cotangent: bfloat16 [256, 65536], P('chan', 'tm'), may hold values from -6 to 6
- silence: int32 [65536], P('tm'), may hold values 0 or 1
- segments: int32 [8192], replicated, may hold values from 0 to 4, as said below
Outputs:
- activation: bfloat16 [256, 65536], P('chan', 'tm')
- input_grad: bfloat16 [512, 8192], P('chan', 'tm')
- up_v_grad: float32 [16, 256, 512], P(None, 'chan')
- up_g_grad: float32 [512], replicated
- up_b_grad: float32 [256], P('chan')
- dilated_direction_gradient: float32 [3, 3, 256, 256], P(None, None, 'chan')
- dil_g_grad: float32 [3, 256], P(None, 'chan')
- dilated_bias_gradient: float32 [3, 256], P(None, 'chan')
- mix_v_grad: float32 [3, 256, 256], P(None, 'chan')
- mix_g_grad: float32 [3, 256], P(None, 'chan')
- out_b_grad: float32 [3, 256], P(None, 'chan')
- skip_v_grad: float32 [3, 256, 256], P(None, 'chan')
- skip_g_grad: float32 [3, 256], P(None, 'chan')
Inputs may be any that keep to these rules, and one draw needn't show every extreme that they name: `segments`: segment numbers of the frames never fall; they rise by one at each segment's first frame, and such rises occur only within the first 1024 and the last 1024 frames (never at frame 0, 1024 or 8192 - 1024).
All inputs are finite; a program needn't handle non-finite values. No bound on the sum of `silence` on one device may be relied on, other than what follows from the above.
Results may differ from a plain program's by a relative error of at most 0.028.
Values may be sent and summed in bfloat16 or wider, within the bound.
No kernel may reach another device: no remote copies, remote signals or barrier semaphores. Data moves between devices by JAX's collectives and lax.ppermute only.
A program may use at most 192 MiB of HBM per device.

v0:
```python
import jax
import jax.numpy as jnp
from jax import lax
from jax.sharding import PartitionSpec as P


def padded(block, sides, width):
    for axis, dim in sides:
        count = lax.axis_size(axis)
        forward = [(i, i + 1) for i in range(count - 1)]
        backward = [(target, source) for source, target in forward]
        low = lax.ppermute(
            lax.slice_in_dim(block, block.shape[dim] - width, None, axis=dim), axis, forward
        )
        high = lax.ppermute(lax.slice_in_dim(block, 0, width, axis=dim), axis, backward)
        block = jnp.concatenate([low, block, high], axis=dim)
    return block


def leaky_soft(values):
    return 0.2 * values + 0.8 * values * jax.nn.sigmoid(values)


def leaky_slope(values):
    sigmoid_v = jax.nn.sigmoid(values)
    return 0.2 + 0.8 * (sigmoid_v + values * sigmoid_v * (1.0 - sigmoid_v))


def matrix_product(form, left_op, right_op):
    return jnp.einsum(form, left_op, right_op, preferred_element_type=jnp.float32)


def weight_normalize(directions, gain_rows, reduce_axes):
    return (
        gain_rows
        * directions
        / jnp.sqrt(jnp.sum(directions * directions, axis=reduce_axes, keepdims=True))
    ).astype(jnp.bfloat16)


def norm_backward(weight_grad, directions, gain_rows, reduce_axes):
    norm_rows = jnp.sqrt(jnp.sum(directions * directions, axis=reduce_axes, keepdims=True))
    inner_dot = jnp.sum(weight_grad * directions, axis=reduce_axes, keepdims=True)
    return (
        gain_rows / norm_rows * weight_grad - gain_rows * inner_dot / norm_rows**3 * directions,
        inner_dot / norm_rows,
    )


def bucket(grad_list, summer):
    flat_grads = jnp.concatenate([piece_grad.reshape(-1) for piece_grad in grad_list])
    summed = summer(flat_grads)
    final_result = []
    offset = 0
    for piece_grad in grad_list:
        final_result.append(summed[offset : offset + piece_grad.size].reshape(piece_grad.shape))
        offset = offset + piece_grad.size
    return final_result


def local(
    spectrogram_input,
    upsample_direction,
    upsample_magnitude,
    upsample_bias,
    dilated_direction,
    dilated_magnitude,
    dilated_bias,
    pointwise_direction,
    pointwise_magnitude,
    block_output_bias,
    shortcut_direction,
    shortcut_magnitude,
    cotangent,
    silence,
    segments,
):
    block_list = dilated_direction.shape[0]

    def extend(values, margin):
        return padded(values, (("tm", 1),), margin)

    def widen(values):
        return lax.all_gather(values, "chan", axis=0, tiled=True)

    def narrow(values):
        return lax.psum_scatter(
            values.astype(jnp.bfloat16), "chan", scatter_dimension=0, tiled=True
        ).astype(jnp.float32)

    def channel_total(values):
        return lax.psum(values, "chan")

    def time_total(values):
        return lax.psum(values.astype(jnp.bfloat16), "tm").astype(jnp.float32)

    def reduce_grads(grad_list):
        return bucket(grad_list, time_total)

    mel_rows, upstream = (spectrogram_input, cotangent)
    (
        stacked_upsample_direction,
        stacked_upsample_bias,
        stacked_dilated_direction,
        stacked_dilated_magnitude,
        stacked_dilated_bias,
    ) = (upsample_direction, upsample_bias, dilated_direction, dilated_magnitude, dilated_bias)
    all_mix_v, all_mix_g, all_out_b, all_skip_v, all_skip_g = (
        pointwise_direction,
        pointwise_magnitude,
        block_output_bias,
        shortcut_direction,
        shortcut_magnitude,
    )
    frame_count = mel_rows.shape[1]
    frame_start = lax.axis_index("tm") * frame_count
    silence_mask_rows = silence.astype(jnp.float32)
    signal_length = 8 * frame_count
    segpad = jnp.pad(segments, 2, constant_values=-1)
    frame_ids = lax.dynamic_slice_in_dim(segpad, frame_start, frame_count + 4)
    left_ok = (frame_ids[1 : frame_count + 1] == frame_ids[2 : frame_count + 2]).astype(jnp.float32)
    right_ok = (frame_ids[3 : frame_count + 3] == frame_ids[2 : frame_count + 2]).astype(
        jnp.float32
    )
    sample_ids = jnp.repeat(frame_ids, 8)

    def same_segment(offset):
        return (
            sample_ids[16 + offset : 16 + offset + signal_length]
            == sample_ids[16 : 16 + signal_length]
        ).astype(jnp.float32)

    up_norm = jnp.sqrt(
        channel_total(jnp.sum(stacked_upsample_direction * stacked_upsample_direction, axis=(0, 1)))
    )
    up_w = (upsample_magnitude * stacked_upsample_direction / up_norm).astype(jnp.bfloat16)
    mel_single_float = mel_rows.astype(jnp.float32)
    mel_ext = widen(extend(leaky_soft(mel_single_float).astype(jnp.bfloat16), 1))
    tap_sums = matrix_product("koi,is->kos", up_w, mel_ext)
    side_terms = jnp.concatenate(
        [
            tap_sums[12:16, :, 0:frame_count] * left_ok,
            tap_sums[0:4, :, 2 : frame_count + 2] * right_ok,
        ],
        axis=0,
    )
    joined = tap_sums[4:12, :, 1 : frame_count + 1] + side_terms
    hidden_state = (
        jnp.transpose(joined, (1, 2, 0)).reshape(joined.shape[1], signal_length)
        + stacked_upsample_bias[:, None]
    )
    saved_state = []
    for dilation_level in range(block_list):
        tap_spacing = 3**dilation_level
        dilated_weight = weight_normalize(
            stacked_dilated_direction[dilation_level],
            stacked_dilated_magnitude[dilation_level][None, :, None],
            (0, 2),
        )
        pointwise_weight = weight_normalize(
            all_mix_v[dilation_level], all_mix_g[dilation_level][:, None], (1,)
        )
        shortcut_weight = weight_normalize(
            all_skip_v[dilation_level], all_skip_g[dilation_level][:, None], (1,)
        )
        hidden_complete = widen(extend(hidden_state.astype(jnp.bfloat16), tap_spacing))
        act_full = leaky_soft(hidden_complete.astype(jnp.float32)).astype(jnp.bfloat16)
        inner_before = stacked_dilated_bias[dilation_level][:, None] + jnp.zeros(
            (dilated_weight.shape[1], signal_length), jnp.float32
        )
        for kernel_offset in range(3):
            inner_before = inner_before + same_segment(
                (kernel_offset - 1) * tap_spacing
            ) * matrix_product(
                "kt,td->kd",
                dilated_weight[kernel_offset],
                act_full[
                    :, kernel_offset * tap_spacing : kernel_offset * tap_spacing + signal_length
                ],
            )
        middle_complete = widen(leaky_soft(inner_before).astype(jnp.bfloat16))
        hidden_state = (
            matrix_product("kt,td->kd", pointwise_weight, middle_complete)
            + matrix_product(
                "kt,td->kd",
                shortcut_weight,
                hidden_complete[:, tap_spacing : tap_spacing + signal_length],
            )
            + all_out_b[dilation_level][:, None]
        )
        saved_state.append(
            (
                hidden_complete,
                inner_before,
                middle_complete,
                dilated_weight,
                pointwise_weight,
                shortcut_weight,
            )
        )
    act_out = (hidden_state * silence_mask_rows).astype(jnp.bfloat16)
    grad_low = (upstream.astype(jnp.float32) * silence_mask_rows).astype(jnp.bfloat16)
    pending = []
    for dilation_level in reversed(range(block_list)):
        tap_spacing = 3**dilation_level
        (
            hidden_complete,
            inner_before,
            middle_complete,
            dilated_weight,
            pointwise_weight,
            shortcut_weight,
        ) = saved_state[dilation_level]
        act_full = leaky_soft(hidden_complete.astype(jnp.float32)).astype(jnp.bfloat16)
        hid_mid = hidden_complete[:, tap_spacing : tap_spacing + signal_length]
        pointwise_gradient = matrix_product("os,is->oi", grad_low, middle_complete)
        shortcut_gradient = matrix_product("os,is->oi", grad_low, hid_mid)
        output_bias_term = jnp.sum(grad_low.astype(jnp.float32), axis=1)
        mid_grad = narrow(matrix_product("qj,qc->jc", pointwise_weight, grad_low))
        inner_lower = (mid_grad * leaky_slope(inner_before)).astype(jnp.bfloat16)
        dilated_bias_term = jnp.sum(inner_lower.astype(jnp.float32), axis=1)
        inner_ext = extend(inner_lower, tap_spacing)
        dilated_gradient = jnp.stack(
            [
                matrix_product(
                    "os,is->oi",
                    inner_lower
                    * same_segment((kernel_offset - 1) * tap_spacing).astype(jnp.bfloat16),
                    act_full[
                        :, kernel_offset * tap_spacing : kernel_offset * tap_spacing + signal_length
                    ],
                )
                for kernel_offset in range(3)
            ]
        )
        spread_input = jnp.zeros((hidden_complete.shape[0], signal_length), jnp.float32)
        for kernel_offset in range(3):
            shifted_rows = inner_ext[
                :,
                (2 - kernel_offset) * tap_spacing : (2 - kernel_offset) * tap_spacing
                + signal_length,
            ] * same_segment((1 - kernel_offset) * tap_spacing).astype(jnp.bfloat16)
            spread_input = spread_input + matrix_product(
                "qj,qc->jc", dilated_weight[kernel_offset], shifted_rows
            )
        total_in = spread_input * leaky_slope(hid_mid.astype(jnp.float32)) + matrix_product(
            "qj,qc->jc", shortcut_weight, grad_low
        )
        grad_low = narrow(total_in).astype(jnp.bfloat16)
        gradient_pieces = [
            dilated_gradient,
            dilated_bias_term,
            pointwise_gradient,
            output_bias_term,
            shortcut_gradient,
        ]
        gradient_pieces = reduce_grads(gradient_pieces)
        pending.insert(0, gradient_pieces)
    grad_ext = extend(grad_low, 8)
    frames_grad = jnp.transpose(grad_ext.reshape(grad_ext.shape[0], frame_count + 2, 8), (2, 0, 1))
    kernel_grad = jnp.concatenate(
        [
            frames_grad[4:8, :, 0:frame_count] * left_ok.astype(jnp.bfloat16),
            frames_grad[:, :, 1 : frame_count + 1],
            frames_grad[0:4, :, 2 : frame_count + 2] * right_ok.astype(jnp.bfloat16),
        ],
        axis=0,
    )
    mel_grad = narrow(matrix_product("koi,kos->is", up_w, kernel_grad))
    grad_out = (mel_grad * leaky_slope(mel_single_float)).astype(jnp.bfloat16)
    up_grad = matrix_product("kos,is->koi", kernel_grad, mel_ext[:, 1 : frame_count + 1])
    up_bias = jnp.sum(grad_low.astype(jnp.float32), axis=1)
    up_grad, up_bias = reduce_grads([up_grad, up_bias])
    channel_groups = [jnp.stack([stored[member] for stored in pending]) for member in range(5)]
    up_dot = channel_total(jnp.sum(up_grad * upsample_direction, axis=(0, 1)))
    up_v_grad = (
        upsample_magnitude / up_norm * up_grad
        - upsample_magnitude * up_dot / up_norm**3 * upsample_direction
    )
    up_g_grad = up_dot / up_norm
    dilated_direction_gradient, dilated_magnitude_saved = norm_backward(
        channel_groups[0], dilated_direction, dilated_magnitude[:, None, :, None], (1, 3)
    )
    dilated_bias_gradient = channel_groups[1]
    mix_v_grad, mix_g_keep = norm_backward(
        channel_groups[2], pointwise_direction, pointwise_magnitude[:, :, None], (2,)
    )
    out_b_grad = channel_groups[3]
    skip_v_grad, skip_g_keep = norm_backward(
        channel_groups[4], shortcut_direction, shortcut_magnitude[:, :, None], (2,)
    )
    return (
        act_out,
        grad_out,
        up_v_grad,
        up_g_grad,
        up_bias,
        dilated_direction_gradient,
        dilated_magnitude_saved[:, 0, :, 0],
        dilated_bias_gradient,
        mix_v_grad,
        mix_g_keep[:, :, 0],
        out_b_grad,
        skip_v_grad,
        skip_g_keep[:, :, 0],
    )


def solution(mesh):
    placed = (
        P("chan", "tm"),
        P(None, "chan", None),
        P(),
        P("chan"),
        P(None, None, "chan", None),
        P(None, "chan"),
        P(None, "chan"),
        P(None, "chan", None),
        P(None, "chan"),
        P(None, "chan"),
        P(None, "chan", None),
        P(None, "chan"),
        P("chan", "tm"),
        P("tm"),
        P(),
    )
    return jax.shard_map(
        local,
        mesh=mesh,
        in_specs=placed,
        out_specs=(
            P("chan", "tm"),
            P("chan", "tm"),
            P(None, "chan", None),
            P(),
            P("chan"),
            P(None, None, "chan", None),
            P(None, "chan"),
            P(None, "chan"),
            P(None, "chan", None),
            P(None, "chan"),
            P(None, "chan"),
            P(None, "chan", None),
            P(None, "chan"),
        ),
        check_vma=False,
    )
```

profile of v0, /device:TPU:0, one launch (start us, length us, event | category | flops | bytes accessed | tf_op | source)
XLA Modules:
  0.0 861.6 jit_solution(7540563130660467685)
XLA Ops:
  9.9 5.5 collective-permute-start
  22.5 5.9 psum.42
  31.3 9.7 %all-gather.8.cloned.1.call-done = bf16[512,1026]{0,1:T(8,128)(2,1)} async-done(((bf16[128,1026]{0,1:T(8,128)(2,1)}), bf16[512,1026]{0,1:T(8,128)(2,1)}) %all-gather.8.cloned.1.call-update) | async-done | bytes 1050640 | tf_op jit(solution)/shard_map/all_gather | solution.py:84
  66.9 33.2 %all-gather.10.cloned.1.call-done = bf16[256,8194]{1,0:T(8,128)(2,1)} async-done(((bf16[64,8194]{1,0:T(8,128)(2,1)}), bf16[256,8194]{1,0:T(8,128)(2,1)}) %all-gather.10.cloned.1.call-update) | async-done | bytes 4195344 | tf_op jit(solution)/shard_map/all_gather | solution.py:84
  113.4 32.2 %all-gather.12.cloned.1.call-done = bf16[256,8192]{1,0:T(8,128)(2,1)} async-done(((bf16[64,8192]{1,0:T(8,128)(2,1)}), bf16[256,8192]{1,0:T(8,128)(2,1)}) %all-gather.12.cloned.1.call-update) | async-done | bytes 4194320 | tf_op jit(solution)/shard_map/all_gather | solution.py:84
  162.9 36.1 %all-gather.14.cloned.1.call-done = bf16[256,8198]{1,0:T(8,128)(2,1)} async-done(((bf16[64,8198]{1,0:T(8,128)(2,1)}), bf16[256,8198]{1,0:T(8,128)(2,1)}) %all-gather.14.cloned.1.call-update) | async-done | bytes 4197392 | tf_op jit(solution)/shard_map/all_gather | solution.py:84
  209.9 34.6 %all-gather.16.cloned.1.call-done = bf16[256,8192]{1,0:T(8,128)(2,1)} async-done(((bf16[64,8192]{1,0:T(8,128)(2,1)}), bf16[256,8192]{1,0:T(8,128)(2,1)}) %all-gather.16.cloned.1.call-update) | async-done | bytes 4194320 | tf_op jit(solution)/shard_map/all_gather | solution.py:84
  265.1 32.9 %all-gather.18.cloned.1.call-done = bf16[256,8210]{1,0:T(8,128)(2,1)} async-done(((bf16[64,8210]{1,0:T(8,128)(2,1)}), bf16[256,8210]{1,0:T(8,128)(2,1)}) %all-gather.18.cloned.1.call-update) | async-done | bytes 4203536 | tf_op jit(solution)/shard_map/all_gather | solution.py:84
  309.0 36.1 %reduce-scatter.10.cloned.1.call-done = bf16[64,8192]{1,0:T(8,128)(2,1)} async-done(((bf16[256,8192]{1,0:T(8,128)(2,1)}), bf16[64,8192]{1,0:T(8,128)(2,1)}) %reduce-scatter.10.cloned.1.call-update) | async-done | bytes 1048592 | tf_op jit(solution)/shard_map/reduce_scatter | solution.py:87
  359.1 8.0 fusion.3
  367.0 6.7 fusion.6
  373.8 44.6 %reduce-scatter.12.cloned.1.call-done = bf16[64,8192]{1,0:T(8,128)(2,1)} async-done(((bf16[256,8192]{1,0:T(8,128)(2,1)}), bf16[64,8192]{1,0:T(8,128)(2,1)}) %reduce-scatter.12.cloned.1.call-update) | async-done | bytes 1048592 | tf_op jit(solution)/shard_map/reduce_scatter | solution.py:87
  423.2 44.6 %reduce-scatter.14.cloned.1.call-done = bf16[64,8192]{1,0:T(8,128)(2,1)} async-done(((bf16[256,8192]{1,0:T(8,128)(2,1)}), bf16[64,8192]{1,0:T(8,128)(2,1)}) %reduce-scatter.14.cloned.1.call-update) | async-done | bytes 1048592 | tf_op jit(solution)/shard_map/reduce_scatter | solution.py:87
  481.7 8.8 %fusion.4 = f32[256,8192]{1,0:T(8,128)} fusion(f32[256,8192]{1,0:T(8,128)S(1)} %fusion.183, f32[256,8192]{1,0:T(8,128)S(1)} %fusion.261, bf16[256,8198]{1,0:T(8,128)(2,1)S(1)} %bitcast.266, bf16[64,3]{1,0:T(8,128)(2,1)S(1)} %collective-permute-done.10, bf16[64,8192]{1,0:T(8,128)(2,1)S(1)} %get-tuple-element.74, bf16[8192]{0:T(1024)(128)(2,1)S(1)} %copy-done.43, ...), kind=kOutput, calls=%fused_computation.19 | convolution fusion | flops 298844160 | bytes 30458240 | tf_op jit(solution)/shard_map/qj,qc->jc/dot_general | solution.py:30
  490.5 6.8 fusion.7
  497.3 44.6 %reduce-scatter.16.cloned.1.call-done = bf16[64,8192]{1,0:T(8,128)(2,1)} async-done(((bf16[256,8192]{1,0:T(8,128)(2,1)}), bf16[64,8192]{1,0:T(8,128)(2,1)}) %reduce-scatter.16.cloned.1.call-update) | async-done | bytes 1048592 | tf_op jit(solution)/shard_map/reduce_scatter | solution.py:87
  547.2 44.1 %reduce-scatter.18.cloned.1.call-done = bf16[64,8192]{1,0:T(8,128)(2,1)} async-done(((bf16[256,8192]{1,0:T(8,128)(2,1)}), bf16[64,8192]{1,0:T(8,128)(2,1)}) %reduce-scatter.18.cloned.1.call-update) | async-done | bytes 1048592 | tf_op jit(solution)/shard_map/reduce_scatter | solution.py:87
  605.3 8.8 %fusion.5 = f32[256,8192]{1,0:T(8,128)} fusion(f32[256,8192]{1,0:T(8,128)S(1)} %fusion.176, f32[256,8192]{1,0:T(8,128)S(1)} %fusion.260, bf16[256,8194]{1,0:T(8,128)(2,1)S(1)} %bitcast.262, bf16[64,1]{1,0:T(8,128)(2,1)S(1)} %collective-permute-done.12, bf16[64,8192]{1,0:T(8,128)(2,1)S(1)} %get-tuple-element.76, bf16[8192]{0:T(1024)(128)(2,1)S(1)} %copy-done.41, ...), kind=kOutput, calls=%fused_computation.20 | convolution fusion | flops 298844160 | bytes 30457984 | tf_op jit(solution)/shard_map/qj,qc->jc/dot_general | solution.py:30
  614.1 6.9 fusion.8
  637.7 5.2 concatenate.74
  685.2 5.9 collective-permute-start.14
  710.8 5.1 fusion.21
  718.2 79.6 %all-reduce.4.cloned.1.call-done = (bf16[524352]{0:T(1024)(128)(2,1)}, bf16[82048]{0:T(1024)(128)(2,1)}, bf16[82048]{0:T(1024)(128)(2,1)}, bf16[82048]{0:T(1024)(128)(2,1)}) async-done(((bf16[524352]{0:T(1024)(128)(2,1)}, bf16[82048]{0:T(1024)(128)(2,1)}, bf16[82048]{0:T(1024)(128)(2,1)}, bf16[82048]{0:T(1024)(128)(2,1)}), (bf16[524352]{0:T(1024)(128)(2,1)}, bf16[82048]{0:T(1024)(128)(2,1)}, ...) | async-done | bytes 1541008 | tf_op jit(solution)/shard_map/psum | solution.py:95
  837.3 6.9 psum.44
  (433 shorter events, 292.8 us)
Async XLA Ops:
  7.2 33.8 %all-gather.8.cloned.1.call-start = ((), (), s32[]{:S(2)}) async-start(), calls=%async_computation.7 | async-start | bytes 1320960 | tf_op jit(solution)/shard_map/all_gather | solution.py:84
  8.6 6.8 collective-permute-start.1
  9.9 6.8 collective-permute-start
  20.6 79.4 %all-gather.10.cloned.1.call-start = ((), (), s32[]{:S(2)}) async-start(), calls=%async_computation.8 | async-start | bytes 5324800 | tf_op jit(solution)/shard_map/all_gather | solution.py:84
  53.8 6.0 collective-permute-start.2
  63.4 82.2 %all-gather.12.cloned.1.call-start = ((), (), s32[]{:S(2)}) async-start(), calls=%async_computation.9 | async-start | bytes 5242880 | tf_op jit(solution)/shard_map/all_gather | solution.py:84
  110.9 88.1 %all-gather.14.cloned.1.call-start = ((), (), s32[]{:S(2)}) async-start(), calls=%async_computation.10 | async-start | bytes 5324800 | tf_op jit(solution)/shard_map/all_gather | solution.py:84
  153.9 6.0 collective-permute-start.4
  162.3 82.1 %all-gather.16.cloned.1.call-start = ((), (), s32[]{:S(2)}) async-start(), calls=%async_computation.11 | async-start | bytes 5242880 | tf_op jit(solution)/shard_map/all_gather | solution.py:84
  209.8 88.2 %all-gather.18.cloned.1.call-start = ((), (), s32[]{:S(2)}) async-start(), calls=%async_computation.12 | async-start | bytes 5324800 | tf_op jit(solution)/shard_map/all_gather | solution.py:84
  261.3 83.8 %reduce-scatter.10.cloned.1.call-start = ((), (), s32[]{:S(2)}) async-start(), calls=%async_computation.14 | async-start | bytes 5242880 | tf_op jit(solution)/shard_map/reduce_scatter | solution.py:87
  264.8 153.6 %reduce-scatter.12.cloned.1.call-start = ((), (), s32[]{:S(2)}) async-start(), calls=%async_computation.15 | async-start | bytes 5242880 | tf_op jit(solution)/shard_map/reduce_scatter | solution.py:87
  348.6 6.3 collective-permute-start.9
  373.8 94.0 %reduce-scatter.14.cloned.1.call-start = ((), (), s32[]{:S(2)}) async-start(), calls=%async_computation.16 | async-start | bytes 5242880 | tf_op jit(solution)/shard_map/reduce_scatter | solution.py:87
  423.1 118.8 %reduce-scatter.16.cloned.1.call-start = ((), (), s32[]{:S(2)}) async-start(), calls=%async_computation.17 | async-start | bytes 5242880 | tf_op jit(solution)/shard_map/reduce_scatter | solution.py:87
  471.4 6.4 collective-permute-start.11
  497.3 93.9 %reduce-scatter.18.cloned.1.call-start = ((), (), s32[]{:S(2)}) async-start(), calls=%async_computation.18 | async-start | bytes 5242880 | tf_op jit(solution)/shard_map/reduce_scatter | solution.py:87
  546.5 87.3 %all-gather.20.cloned.1.call-start = ((), (), s32[]{:S(2)}) async-start(), calls=%async_computation.13 | async-start | bytes 5242880 | tf_op jit(solution)/shard_map/all_gather | solution.py:84
  547.1 136.0 %reduce-scatter.20.cloned.1.call-start = ((), (), s32[]{:S(2)}) async-start(), calls=%async_computation.19 | async-start | bytes 5242880 | tf_op jit(solution)/shard_map/reduce_scatter | solution.py:87
  594.8 6.3 collective-permute-start.13
  621.0 176.9 %all-reduce.4.cloned.1.call-start = ((), (), s32[]{:S(2)}) async-start(), calls=%async_computation.21 | async-start | bytes 3096576 | tf_op jit(solution)/shard_map/psum | solution.py:95
  683.9 12.8 %collective-permute-start.15 = (bf16[64,8]{1,0:T(8,128)(2,1)S(1)}, bf16[64,8]{1,0:T(8,128)(2,1)S(1)}, u32[]{:S(2)}, u32[]{:S(2)}) collective-permute-start(bf16[64,8]{1,0:T(8,128)(2,1)S(1)} %get-tuple-element.98), channel_id=1, source_target_pairs={{4,0},{8,4},{12,8},{16,12},{20,16},{24,20},{28,24},{5,1},{9,5},{13... | collective-permute-start | bytes 3080 | tf_op jit(solution)/shard_map/ppermute | solution.py:15
  685.2 11.5 %collective-permute-start.14 = (bf16[64,8]{1,0:T(8,128)(2,1)S(1)}, bf16[64,8]{1,0:T(8,128)(2,1)S(1)}, u32[]{:S(2)}, u32[]{:S(2)}) collective-permute-start(bf16[64,8]{1,0:T(8,128)(2,1)S(1)} %get-tuple-element.99), channel_id=1, source_target_pairs={{0,4},{4,8},{8,12},{12,16},{16,20},{20,24},{24,28},{1,5},{5,9},{9,... | collective-permute-start | bytes 3080 | tf_op jit(solution)/shard_map/ppermute | solution.py:12
  707.4 145.2 %reduce-scatter.22.cloned.1.call-start = ((), (), s32[]{:S(2)}) async-start(), calls=%async_computation.20 | async-start | bytes 1310720
  (105 other events, 1403.5 us)
Sparse Core Ops, SparseCore 0:
  20.8 20.1 all-gather.7
  63.5 36.5 all-gather.9
  111.0 34.4 all-gather.11
  162.4 36.5 all-gather.13
  209.9 34.4 all-gather.15
  261.4 36.5 all-gather.17
  300.5 44.4 reduce-scatter.9
  373.9 44.5 reduce-scatter.11
  423.2 44.5 reduce-scatter.13
  497.4 44.4 reduce-scatter.15
  546.7 44.5 reduce-scatter.17
  593.3 34.4 all-gather.19
  630.5 44.5 reduce-scatter.19
  707.5 90.3 all-reduce.3
  800.3 24.2 reduce-scatter.21
where the time goes:
time: 868 us; the launch traced here: 862 us
  waiting for transfers between devices  487 us (56%)
  matrix products  165 us (19%)
  local copies, waits for them, and re-layouts  80.9 us (9%)
  other arithmetic  51.7 us (6%)
  starting transfers between devices  48.2 us (6%)
  between operations  16 us (2%)
  blocking collectives  12.8 us (1%)
    reduce_scatter x6, waiting for transfers between devices, narrow(): lax.psum_scatter(values.astype(jnp.bfloat16), 'chan', scatter_dimension=0...  214 us
    all_gather x7, waiting for transfers between devices, widen(): return lax.all_gather(values, 'chan', axis=0, tiled=True)  179 us
    dot_general x48, matrix products, matrix_product(): jnp.einsum(form, left_op, right_op, preferred_element_type=jnp.float32)  165 us
    psum x1, waiting for transfers between devices, time_total(): return lax.psum(values.astype(jnp.bfloat16), 'tm').astype(jnp.float32)  79.6 us
    ppermute x8, starting transfers between devices, padded(): lax.ppermute(lax.slice_in_dim(block, block.shape[dim] - width, None, axis...  35.2 us
  transfers between devices with their start and end apart: 31, of which 19 were waited for; matrix products, arithmetic and copies ran while one was open for 20% of the time, Pallas kernels for 0%

commit v1 on v0

v1 whole, which is shorter than its diff:
```python
import functools

import jax
import jax.numpy as jnp
from jax import lax
from jax.experimental import pallas as pl
from jax.experimental.pallas import tpu as pltpu
from jax.sharding import PartitionSpec as P

BF = jnp.bfloat16
F32 = jnp.float32
LANES = 128
HALO = 128
CHUNK = 256
TAIL = 128
VMEM_LIMIT = 60 * 1024 * 1024


def swap(values, axis, bit):
    count = lax.axis_size(axis)
    return lax.ppermute(values, axis, [(k, k ^ bit) for k in range(count)])


def bits_of(count):
    bits = []
    bit = 1
    while bit < count:
        bits.append(bit)
        bit = 2 * bit
    return bits


def add_low(*terms):
    total = terms[0].astype(F32)
    for term in terms[1:]:
        total = total + term.astype(F32)
    return total.astype(BF)


def gather_chan(own):
    held = {0: own}
    for bit in reversed(bits_of(lax.axis_size("chan"))):
        for slot in list(held):
            held[slot ^ bit] = swap(held[slot], "chan", bit)
    return [held[slot] for slot in range(len(held))]


def exchange_chan(pieces):
    return [pieces[0]] + [swap(pieces[s], "chan", s) for s in range(1, len(pieces))]


def scatter_chan(pieces):
    held = dict(enumerate(pieces))
    for bit in bits_of(len(pieces)):
        for slot in sorted(held):
            if slot & bit:
                held[slot ^ bit] = add_low(held[slot ^ bit], swap(held[slot], "chan", bit))
        held = {slot: piece for slot, piece in held.items() if not slot & bit}
    return held[0]


def kernel_call(body, outs, args, scratch=(), flops=0, specs=None):
    if specs is None:
        specs = [None] * len(args)
    in_specs = [
        pl.BlockSpec(memory_space=pltpu.VMEM) if spec is None else spec for spec in specs
    ]
    moved = sum(a.size * a.dtype.itemsize for a in args)
    moved = moved + sum(o.size * o.dtype.itemsize for o in outs)
    return pl.pallas_call(
        body,
        out_shape=tuple(outs),
        in_specs=in_specs,
        out_specs=tuple(pl.BlockSpec(memory_space=pltpu.VMEM) for _ in outs),
        scratch_shapes=list(scratch),
        compiler_params=pltpu.CompilerParams(vmem_limit_bytes=VMEM_LIMIT),
        cost_estimate=pl.CostEstimate(
            flops=int(flops), bytes_accessed=int(moved), transcendentals=0
        ),
    )(*args)


SMEM = pl.BlockSpec(memory_space=pltpu.SMEM)


def shaped(shape, dtype):
    return jax.ShapeDtypeStruct(shape, dtype)


def unit(values):
    th = jnp.tanh(0.5 * values)
    base = 0.6 + 0.4 * th
    return values * base, base + 0.2 * values * (1.0 - th * th)


def unit_act(values):
    return values * (0.6 + 0.4 * jnp.tanh(0.5 * values))


def dot(left, right):
    return lax.dot_general(left, right, (((1,), (0,)), ((), ())), preferred_element_type=F32)


def dot_rt(left, right):
    return lax.dot_general(left, right, (((1,), (1,)), ((), ())), preferred_element_type=F32)


def eye_mask(count):
    rows = lax.broadcasted_iota(jnp.int32, (count, count), 0)
    cols = lax.broadcasted_iota(jnp.int32, (count, count), 1)
    return rows == cols


def to_col(row, eye):
    return jnp.sum(jnp.where(eye, row, 0.0), axis=1, keepdims=True)


def to_row(col, eye):
    return jnp.sum(jnp.where(eye, col, 0.0), axis=0, keepdims=True)


def at(start, size, step):
    return pl.ds(pl.multiple_of(start, step), size)


def prep_kernel(
    up_v, dil_v, dil_g, dil_b, mix_v, mix_g, out_b, skip_v, skip_g, cot, sil,
    up_sq, packed, order, left_edge, right_edge,
):
    taps = up_v.shape[0]
    local_out = up_v.shape[1]
    total = jnp.zeros((1, up_v.shape[2]), F32)
    for k in range(taps):
        rows = up_v[k]
        total = total + jnp.sum(rows * rows, axis=0, keepdims=True)
    up_sq[...] = total
    eye = eye_mask(local_out)
    lane = lax.broadcasted_iota(jnp.int32, (local_out, TAIL), 1)
    width = dil_v.shape[3]
    for j in range(dil_v.shape[0]):
        rows = pl.ds(j * local_out, local_out)
        square = jnp.zeros((local_out, 1), F32)
        for k in range(3):
            v = dil_v[j, k]
            square = square + jnp.sum(v * v, axis=1, keepdims=True)
        norm = jnp.sqrt(square)
        gain = to_col(dil_g[j : j + 1, :], eye)
        for k in range(3):
            packed[rows, k * width : (k + 1) * width] = (gain * dil_v[j, k] / norm).astype(BF)
        for number, (vref, gref) in enumerate(((mix_v, mix_g), (skip_v, skip_g))):
            v = vref[j]
            norm = jnp.sqrt(jnp.sum(v * v, axis=1, keepdims=True))
            gain = to_col(gref[j : j + 1, :], eye)
            packed[rows, (3 + number) * width : (4 + number) * width] = (gain * v / norm).astype(BF)
        first = to_col(dil_b[j : j + 1, :], eye)
        second = to_col(out_b[j : j + 1, :], eye)
        high_one = first.astype(BF).astype(F32)
        high_two = second.astype(BF).astype(F32)
        tail = jnp.where(lane == 0, high_one, 0.0) + jnp.where(lane == 1, first - high_one, 0.0)
        tail = tail + jnp.where(lane == 2, high_two, 0.0)
        tail = tail + jnp.where(lane == 3, second - high_two, 0.0)
        packed[rows, 5 * width : 5 * width + TAIL] = tail.astype(BF)
    size = order.shape[0]
    source = lax.broadcasted_iota(jnp.int32, (size, size), 0)
    target = lax.broadcasted_iota(jnp.int32, (size, size), 1)
    hit = target == 8 * (source & (LANES - 1)) + (source >> 7)
    order[...] = jnp.where(hit, 1.0, 0.0).astype(BF)
    count = cot.shape[1]
    left_edge[...] = (
        cot[:, 0:HALO].astype(F32) * sil[:, 0:HALO].astype(F32)
    ).astype(BF)
    right_edge[...] = (
        cot[:, count - HALO : count].astype(F32) * sil[:, count - HALO : count].astype(F32)
    ).astype(BF)


def cut_kernel(pieces, idx, cot, sil, low, high, *refs):
    outs, wide = refs[:pieces], refs[pieces]
    count = cot.shape[1]
    own = count // pieces
    wide[:, 0:HALO] = low[...]
    wide[:, HALO : HALO + count] = (cot[...].astype(F32) * sil[...].astype(F32)).astype(BF)
    wide[:, HALO + count :] = high[...]
    for s in range(pieces):
        peer = idx[1] ^ s
        outs[s][...] = wide[:, at(peer * own, own + 2 * HALO, LANES)]


def weight_kernel(pieces, blocks, idx, *refs):
    parts, (plain, dil_t, point_t) = refs[:pieces], refs[pieces:]
    rows = parts[0].shape[0] // blocks
    for s in range(pieces):
        start = (idx[1] ^ s) * rows
        for j in range(blocks):
            plain[j, at(start, rows, 16), :] = parts[s][j * rows : (j + 1) * rows, :]
    width = plain.shape[1]
    for j in range(blocks):
        for k in range(5):
            turned = jnp.transpose(plain[j, :, k * width : (k + 1) * width])
            if k < 3:
                dil_t[j, :, k * width : (k + 1) * width] = turned
            else:
                point_t[j, :, (k - 3) * width : (k - 2) * width] = turned


def up_kernel(pieces, idx, *refs):
    mains, sides = refs[:pieces], refs[pieces : 2 * pieces]
    up_v, up_sq, up_g, up_b, frame_id, order = refs[2 * pieces : 2 * pieces + 6]
    outs = refs[2 * pieces + 6 : 3 * pieces + 6]
    act_out, up_w = refs[3 * pieces + 6 : 3 * pieces + 8]
    raw, stacked, phases, wide = refs[3 * pieces + 8 :]
    rows, frames = mains[0].shape
    local_out = up_v.shape[1]
    for s in range(pieces):
        here = at((idx[1] ^ s) * rows, rows, 16)
        raw[here, 0:LANES] = sides[s][:, 0:LANES]
        raw[here, LANES : LANES + frames] = mains[s][...]
        raw[here, LANES + frames :] = sides[s][:, LANES:]
    scale = up_g[...] / jnp.sqrt(up_sq[...])
    norm = jnp.sqrt(up_sq[...])
    for k in range(up_v.shape[0]):
        up_w[k * local_out : (k + 1) * local_out, :] = (up_g[...] * up_v[k] / norm).astype(BF)
    del scale
    total = frames + 2 * LANES
    count = stacked.shape[1]
    channels = raw.shape[0]
    shift = total - (LANES - HALO // 8)
    ids = pltpu.roll(jnp.broadcast_to(frame_id[...], (8, total)), shift, axis=1)
    before = pltpu.roll(ids, 1, axis=1)
    after = pltpu.roll(ids, total - 1, axis=1)
    left = jnp.where(before == ids, 1.0, 0.0)[0:1, :]
    right = jnp.where(after == ids, 1.0, 0.0)[0:1, :]
    step = LANES
    for r0 in range(0, channels, step):
        part = pl.ds(r0, step)
        acted = unit_act(raw[part, :].astype(F32)).astype(BF)
        act_out[part, :] = acted[:, LANES : LANES + frames]
        moved = pltpu.roll(acted, shift, axis=1)
        one = pltpu.roll(moved, 1, axis=1).astype(F32) * left
        two = pltpu.roll(moved, total - 1, axis=1).astype(F32) * right
        stacked[part, :] = moved[:, 0:count]
        stacked[pl.ds(channels + r0, step), :] = one[:, 0:count].astype(BF)
        stacked[pl.ds(2 * channels + r0, step), :] = two[:, 0:count].astype(BF)
    eye = eye_mask(local_out)
    bias = to_col(up_b[...], eye)
    bias4 = jnp.concatenate([bias] * 4, axis=0)
    quarter = 4 * local_out
    for c0 in range(0, count, 3 * LANES):
        cols = pl.ds(c0, 3 * LANES)
        center = stacked[0:channels, cols]
        low = dot(up_w[quarter : 2 * quarter, :], center)
        low = low + dot(up_w[3 * quarter : 4 * quarter, :], stacked[channels : 2 * channels, cols])
        high = dot(up_w[2 * quarter : 3 * quarter, :], center)
        high = high + dot(up_w[0:quarter, :], stacked[2 * channels : 3 * channels, cols])
        low = (low + bias4).astype(BF)
        high = (high + bias4).astype(BF)
        for b in range(3):
            block = c0 // LANES + b
            if block * local_out >= phases.shape[0]:
                continue
            for r in range(8):
                source = (low, high)[r // 4]
                phases[block * local_out : (block + 1) * local_out, r * LANES : (r + 1) * LANES] = (
                    source[
                        (r % 4) * local_out : (r % 4 + 1) * local_out,
                        b * LANES : (b + 1) * LANES,
                    ]
                )
    for block in range(count // LANES):
        piece = dot(phases[block * local_out : (block + 1) * local_out, :], order[...])
        wide[:, block * 1024 : (block + 1) * 1024] = piece.astype(BF)
    own = 8 * frames // pieces
    for s in range(pieces):
        outs[s][...] = wide[:, at((idx[1] ^ s) * own, own + 2 * HALO, LANES)]


def sample_masks(sample_id, distance):
    width = sample_id.shape[1]
    ids = jnp.broadcast_to(sample_id[...], (8, width))
    back = pltpu.roll(ids, distance, axis=1)
    ahead = pltpu.roll(ids, width - distance, axis=1)
    return (
        jnp.where(back == ids, 1.0, 0.0)[0:1, :].astype(BF),
        jnp.where(ahead == ids, 1.0, 0.0)[0:1, :].astype(BF),
    )


def forward_kernel(pieces, blocks, idx, *refs):
    parts = refs[:pieces]
    plain, sample_id, silence = refs[pieces : pieces + 3]
    outs = refs[pieces + 3 : 2 * pieces + 3]
    kept = refs[2 * pieces + 3 : 2 * pieces + 8]
    hidden, taps, pair, final = refs[2 * pieces + 8 :]
    keep_h, keep_u, keep_m, keep_sh, keep_sc = kept
    rows, width = parts[0].shape
    channels = pieces * rows
    for s in range(pieces):
        hidden[at((idx[1] ^ s) * rows, rows, 16), :] = parts[s][...]
    chunks = width // CHUNK
    for j in range(blocks):
        distance = 3**j
        tail = plain[j, :, 5 * channels : 5 * channels + TAIL].astype(F32)
        dil_b = tail[:, 0:1] + tail[:, 1:2]
        out_b = tail[:, 2:3] + tail[:, 3:4]

        def first(i, carry):
            cols = at(i * CHUNK, CHUNK, CHUNK)
            low = hidden[:, cols]
            keep_h[j, :, cols] = low
            pair[channels : 2 * channels, cols] = low
            acted, slope = unit(low.astype(F32))
            acted = acted.astype(BF)
            taps[channels : 2 * channels, cols] = acted
            keep_u[j, :, cols] = acted
            keep_sh[j, :, cols] = slope.astype(BF)
            return carry

        lax.fori_loop(0, chunks, first, 0)
        back, ahead = sample_masks(sample_id, distance)
        center = taps[channels : 2 * channels, :]
        taps[0:channels, :] = pltpu.roll(center, distance, axis=1) * back
        taps[2 * channels : 3 * channels, :] = pltpu.roll(center, width - distance, axis=1) * ahead

        def second(i, carry):
            cols = at(i * CHUNK, CHUNK, CHUNK)
            inner = dot(plain[j, :, 0 : 3 * channels], taps[:, cols]) + dil_b
            acted, slope = unit(inner)
            acted = acted.astype(BF)
            pair[0:channels, cols] = acted
            keep_m[j, :, cols] = acted
            keep_sc[j, :, cols] = slope.astype(BF)
            after = dot(plain[j, :, 3 * channels : 5 * channels], pair[:, cols]) + out_b
            if j < blocks - 1:
                hidden[:, cols] = after.astype(BF)
            else:
                final[:, cols] = after
            return carry

        lax.fori_loop(0, chunks, second, 0)
    own = width - 2 * HALO
    voiced = silence[:, at(idx[1] * own, own, LANES)].astype(F32)
    for s in range(pieces):
        here = at((idx[1] ^ s) * rows, rows, 16)
        outs[s][...] = (final[here, HALO : HALO + own] * voiced).astype(BF)


def backward_kernel(pieces, blocks, idx, *refs):
    parts = refs[:pieces]
    dil_t, point_t, sample_id = refs[pieces : pieces + 3]
    keep_h, keep_u, keep_m, keep_sh, keep_sc = refs[pieces + 3 : pieces + 8]
    outs = refs[pieces + 8 : 2 * pieces + 8]
    grads = refs[2 * pieces + 8 : 3 * pieces + 8]
    err, taps, packed = refs[3 * pieces + 8 :]
    rows, width = parts[0].shape
    channels = pieces * rows
    own = width - 2 * HALO
    for s in range(pieces):
        err[at((idx[1] ^ s) * rows, rows, 16), :] = parts[s][...]
    chunks = width // CHUNK
    lane = lax.broadcasted_iota(jnp.int32, (channels, TAIL), 1)
    for j in reversed(range(blocks)):
        distance = 3**j

        def first(i, carry):
            cols = at(i * CHUNK, CHUNK, CHUNK)
            inner = dot(point_t[j, :, 0:channels], err[:, cols])
            inner = inner * keep_sc[j, :, cols].astype(F32)
            taps[channels : 2 * channels, cols] = inner.astype(BF)
            return carry

        lax.fori_loop(0, chunks, first, 0)
        back, ahead = sample_masks(sample_id, distance)
        center = taps[channels : 2 * channels, :]
        taps[0:channels, :] = pltpu.roll(center, width - distance, axis=1) * ahead
        taps[2 * channels : 3 * channels, :] = pltpu.roll(center, distance, axis=1) * back
        inside = pl.ds(HALO, own)
        err_own = err[:, inside]
        packed[:, 3 * channels : 4 * channels] = dot_rt(err_own, keep_m[j, :, inside]).astype(BF)
        packed[:, 4 * channels : 5 * channels] = dot_rt(err_own, keep_h[j, :, inside]).astype(BF)
        for k in range(3):
            packed[:, k * channels : (k + 1) * channels] = dot_rt(
                taps[k * channels : (k + 1) * channels, inside], keep_u[j, :, inside]
            ).astype(BF)
        out_sum = jnp.sum(err_own.astype(F32), axis=1, keepdims=True)
        dil_sum = jnp.sum(
            taps[channels : 2 * channels, inside].astype(F32), axis=1, keepdims=True
        )
        packed[:, 5 * channels : 5 * channels + TAIL] = (
            jnp.where(lane == 0, dil_sum, 0.0) + jnp.where(lane == 1, out_sum, 0.0)
        ).astype(BF)
        for s in range(pieces):
            grads[s][j * rows : (j + 1) * rows, :] = packed[at((idx[1] ^ s) * rows, rows, 16), :]

        def second(i, carry):
            cols = at(i * CHUNK, CHUNK, CHUNK)
            spread = dot(dil_t[j], taps[:, cols]) * keep_sh[j, :, cols].astype(F32)
            spread = spread + dot(point_t[j, :, channels : 2 * channels], err[:, cols])
            err[:, cols] = spread.astype(BF)
            return carry

        lax.fori_loop(0, chunks, second, 0)
    for s in range(pieces):
        outs[s][...] = err[at((idx[1] ^ s) * rows, rows, 16), :]


def up_back_kernel(pieces, peers, split, idx, *refs):
    parts = refs[:pieces]
    up_w, up_v, acted, frame_id, order = refs[pieces : pieces + 5]
    outs = refs[pieces + 5 :]
    half = peers // 2
    sums = outs[0]
    inputs = outs[1 : 1 + pieces]
    near = outs[1 + pieces : 1 + pieces + half]
    far = outs[1 + pieces + half]
    extra = 1 if split else 0
    duo = outs[2 + pieces + half : 2 + pieces + half + half * extra]
    wide, phases, cols_grad, weight_grad, low_grad = outs[2 + pieces + half + half * extra :]
    rows, width = parts[0].shape
    own = width - 2 * HALO
    length = pieces * own
    frames = length // 8
    wide[:, HALO + length :] = jnp.zeros((rows, wide.shape[1] - HALO - length), BF)
    for s in range(pieces):
        peer = idx[1] ^ s
        wide[:, at(HALO + peer * own, own, LANES)] = parts[s][:, HALO : HALO + own]

        @pl.when(peer == 0)
        def _():
            wide[:, 0:HALO] = parts[s][:, 0:HALO]

        @pl.when(peer == pieces - 1)
        def _():
            wide[:, HALO + length : 2 * HALO + length] = parts[s][:, HALO + own :]

    total = wide.shape[1] // 8
    for block in range(total // LANES):
        turned = dot_rt(wide[:, block * 1024 : (block + 1) * 1024], order[...]).astype(BF)
        for r in range(8):
            phases[r * rows : (r + 1) * rows, block * LANES : (block + 1) * LANES] = turned[
                :, r * LANES : (r + 1) * LANES
            ]
    ids = jnp.broadcast_to(frame_id[...], (8, frame_id.shape[1]))
    before = pltpu.roll(ids, 1, axis=1)
    after = pltpu.roll(ids, frame_id.shape[1] - 1, axis=1)
    inside = slice(LANES, LANES + frames)
    left = jnp.where(before == ids, 1.0, 0.0)[0:1, inside]
    right = jnp.where(after == ids, 1.0, 0.0)[0:1, inside]
    lead = HALO // 8
    eighth = 4 * rows
    sample_sum = jnp.zeros((rows, 1), F32)
    for part in range(2):
        base = phases[part * eighth : (part + 1) * eighth, :]
        center = pltpu.roll(base, total - lead, axis=1)[:, 0:frames]
        cols_grad[(4 + 4 * part) * rows : (8 + 4 * part) * rows, :] = center
        partial = jnp.sum(center.astype(F32), axis=1, keepdims=True)
        for r in range(4):
            sample_sum = sample_sum + partial[r * rows : (r + 1) * rows]
        if part == 1:
            moved = pltpu.roll(base, total - lead + 1, axis=1)[:, 0:frames]
            cols_grad[0:eighth, :] = (moved.astype(F32) * left).astype(BF)
        else:
            moved = pltpu.roll(base, total - lead - 1, axis=1)[:, 0:frames]
            cols_grad[12 * rows : 16 * rows, :] = (moved.astype(F32) * right).astype(BF)
    taps = up_v.shape[0]
    step = taps * rows // 4
    channels = up_v.shape[2]
    inner = jnp.zeros((1, channels), F32)
    for q in range(4):
        here = pl.ds(q * step, step)
        grad = dot_rt(cols_grad[here, :], acted[...])
        low_grad[here, :] = grad.astype(BF)
        for k in range(taps // 4):
            inner = inner + jnp.sum(
                grad[k * rows : (k + 1) * rows] * up_v[q * taps // 4 + k], axis=0, keepdims=True
            )
    sums[:, 0:channels] = inner
    sums[:, channels:] = jnp.zeros((1, sums.shape[1] - channels), F32)
    eye = eye_mask(rows)
    sums[:, channels : channels + rows] = to_row(sample_sum, eye)
    first = near[0].shape[0]
    for h in range(half):
        near[h][...] = low_grad[at((idx[0] ^ (2 * h)) * first, first, 16), :]
        far[h] = low_grad[at((idx[0] ^ (2 * h + 1)) * first, first, 16), :]
    if split:
        second = duo[0].shape[1]
        for h in range(half):
            for b in range(2):
                start = peers * first + (idx[0] ^ (2 * h + b)) * second
                duo[h][b] = low_grad[at(start, second, 16), :]
    for f in range(0, frames, CHUNK):
        cols = pl.ds(f, CHUNK)
        weight_grad[:, cols] = lax.dot_general(
            up_w[...], cols_grad[:, cols], (((0,), (0,)), ((), ())), preferred_element_type=F32
        ).astype(BF)
    piece = channels // pieces
    for s in range(pieces):
        inputs[s][...] = weight_grad[at((idx[1] ^ s) * piece, piece, 16), :]


def up_final_kernel(peers, split, idx, *refs):
    half = peers // 2
    firsts, others = refs[:half], refs[half]
    duo = refs[half + 1 : half + 1 + (half if split else 0)]
    up_v, up_sq, up_g, sums, up_v_grad, up_g_grad, whole = refs[
        half + 1 + (half if split else 0) :
    ]
    first = firsts[0].shape[0]
    for h in range(half):
        whole[at((idx[0] ^ (2 * h)) * first, first, 16), :] = firsts[h][...]
        whole[at((idx[0] ^ (2 * h + 1)) * first, first, 16), :] = others[h]
    if split:
        second = duo[0].shape[1]
        for h in range(half):
            for b in range(2):
                start = peers * first + (idx[0] ^ (2 * h + b)) * second
                whole[at(start, second, 16), :] = duo[h][b]
    channels = up_v.shape[2]
    norm = jnp.sqrt(up_sq[...])
    inner = sums[:, 0:channels]
    scale = up_g[...] / norm
    pull = up_g[...] * inner / (norm * norm * norm)
    rows = up_v.shape[1]
    for k in range(up_v.shape[0]):
        grad = whole[k * rows : (k + 1) * rows, :].astype(F32)
        up_v_grad[k] = scale * grad - pull * up_v[k]
    up_g_grad[...] = inner / norm


def block_final_kernel(count, idx, *refs):
    parts = refs[:count]
    dil_v, dil_g, mix_v, mix_g, skip_v, skip_g = refs[count : count + 6]
    outs = refs[count + 6 : count + 14]
    whole = refs[count + 14]
    dil_v_out, dil_g_out, dil_b_out, mix_v_out, mix_g_out, out_b_out, skip_v_out, skip_g_out = outs
    size = parts[0].shape[0]
    for h in range(count):
        whole[at(((idx[0] >> 1) ^ h) * size, size, 16), :] = parts[h][...]
    rows, width = dil_v.shape[2], dil_v.shape[3]
    eye = eye_mask(rows)
    for j in range(dil_v.shape[0]):
        here = pl.ds(j * rows, rows)
        square = jnp.zeros((rows, 1), F32)
        inner = jnp.zeros((rows, 1), F32)
        for k in range(3):
            v = dil_v[j, k]
            grad = whole[here, k * width : (k + 1) * width].astype(F32)
            square = square + jnp.sum(v * v, axis=1, keepdims=True)
            inner = inner + jnp.sum(v * grad, axis=1, keepdims=True)
        norm = jnp.sqrt(square)
        gain = to_col(dil_g[j : j + 1, :], eye)
        for k in range(3):
            grad = whole[here, k * width : (k + 1) * width].astype(F32)
            dil_v_out[j, k] = gain / norm * grad - gain * inner / (norm**3) * dil_v[j, k]
        dil_g_out[j : j + 1, :] = to_row(inner / norm, eye)
        for number, (vref, gref, v_out, g_out) in enumerate(
            ((mix_v, mix_g, mix_v_out, mix_g_out), (skip_v, skip_g, skip_v_out, skip_g_out))
        ):
            v = vref[j]
            grad = whole[here, (3 + number) * width : (4 + number) * width].astype(F32)
            norm = jnp.sqrt(jnp.sum(v * v, axis=1, keepdims=True))
            inner = jnp.sum(v * grad, axis=1, keepdims=True)
            gain = to_col(gref[j : j + 1, :], eye)
            v_out[j] = gain / norm * grad - gain * inner / (norm**3) * v
            g_out[j : j + 1, :] = to_row(inner / norm, eye)
        tail = whole[here, 5 * width : 5 * width + TAIL].astype(F32)
        dil_b_out[j : j + 1, :] = to_row(tail[:, 0:1], eye)
        out_b_out[j : j + 1, :] = to_row(tail[:, 1:2], eye)


def join_kernel(pieces, idx, *refs):
    parts, out = refs[:pieces], refs[pieces]
    own = parts[0].shape[1]
    for s in range(pieces):
        out[:, at((idx[1] ^ s) * own, own, LANES)] = parts[s][...]


def input_kernel(*refs):
    *terms, spectrogram, out = refs
    total = terms[0][...].astype(F32)
    for term in terms[1:]:
        total = total + term[...].astype(F32)
    out[...] = (total * unit(spectrogram[...].astype(F32))[1]).astype(BF)


def local(
    spectrogram_input,
    upsample_direction,
    upsample_magnitude,
    upsample_bias,
    dilated_direction,
    dilated_magnitude,
    dilated_bias,
    pointwise_direction,
    pointwise_magnitude,
    block_output_bias,
    shortcut_direction,
    shortcut_magnitude,
    cotangent,
    silence,
    segments,
):
    pieces, peers = lax.axis_size("chan"), lax.axis_size("tm")
    chan, tm = lax.axis_index("chan"), lax.axis_index("tm")
    idx = jnp.stack([tm, chan]).astype(jnp.int32)
    in_rows, frames = spectrogram_input.shape
    taps, rows, in_channels = upsample_direction.shape
    blocks = dilated_direction.shape[0]
    channels = dilated_direction.shape[3]
    length = 8 * frames
    own = length // pieces
    width = own + 2 * HALO
    packed_width = 5 * channels + TAIL
    half = peers // 2
    forward = [(k, k + 1) for k in range(peers - 1)]
    backward = [(k + 1, k) for k in range(peers - 1)]

    sides = jnp.concatenate(
        [
            lax.ppermute(spectrogram_input[:, frames - LANES :], "tm", forward),
            lax.ppermute(spectrogram_input[:, :LANES], "tm", backward),
        ],
        axis=1,
    )
    all_mains = gather_chan(spectrogram_input)
    all_sides = gather_chan(sides)
    silence_row = silence.reshape(1, length)
    padded_ids = jnp.pad(segments.astype(F32), LANES, constant_values=-1.0)
    frame_id = lax.dynamic_slice_in_dim(padded_ids, tm * frames, frames + 2 * LANES)
    lead = HALO // 8
    sample_id = jnp.repeat(
        lax.dynamic_slice_in_dim(
            padded_ids, LANES + tm * frames + chan * (own // 8) - lead, width // 8
        ),
        8,
    ).reshape(1, width)
    frame_id = frame_id.reshape(1, frames + 2 * LANES)

    up_sq, packed, order, left_edge, right_edge = kernel_call(
        prep_kernel,
        [
            shaped((1, in_channels), F32),
            shaped((blocks * rows, packed_width), BF),
            shaped((8 * LANES, 8 * LANES), BF),
            shaped((rows, HALO), BF),
            shaped((rows, HALO), BF),
        ],
        [
            upsample_direction,
            dilated_direction,
            dilated_magnitude,
            dilated_bias,
            pointwise_direction,
            pointwise_magnitude,
            block_output_bias,
            shortcut_direction,
            shortcut_magnitude,
            cotangent,
            silence_row,
        ],
    )
    up_sq = lax.psum(up_sq, "chan")
    up_g = upsample_magnitude.reshape(1, in_channels)
    low_edge = lax.ppermute(right_edge, "tm", forward)
    high_edge = lax.ppermute(left_edge, "tm", backward)

    all_packed = gather_chan(packed)
    count = -(-(frames + 2 * lead) // LANES) * LANES
    count = -(-count // (3 * LANES)) * 3 * LANES
    up_outs = kernel_call(
        functools.partial(up_kernel, pieces),
        [shaped((rows, width), BF)] * pieces
        + [shaped((in_channels, frames), BF), shaped((taps * rows, in_channels), BF)],
        [idx]
        + all_mains
        + all_sides
        + [upsample_direction, up_sq, up_g, upsample_bias.reshape(1, rows), frame_id, order],
        scratch=[
            pltpu.VMEM((in_channels, frames + 2 * LANES), BF),
            pltpu.VMEM((3 * in_channels, count), BF),
            pltpu.VMEM((count // LANES * rows, 8 * LANES), BF),
            pltpu.VMEM((rows, 8 * count), BF),
        ],
        flops=2 * taps * rows * in_channels * count,
        specs=[SMEM] + [None] * (2 * pieces + 6),
    )
    acted, up_w = up_outs[pieces:]
    all_hidden = exchange_chan(list(up_outs[:pieces]))

    plain, dil_t, point_t = kernel_call(
        functools.partial(weight_kernel, pieces, blocks),
        [
            shaped((blocks, channels, packed_width), BF),
            shaped((blocks, channels, 3 * channels), BF),
            shaped((blocks, channels, 2 * channels), BF),
        ],
        [idx] + all_packed,
        specs=[SMEM] + [None] * pieces,
    )
    cut = kernel_call(
        functools.partial(cut_kernel, pieces),
        [shaped((rows, width), BF)] * pieces,
        [idx, cotangent, silence_row, low_edge, high_edge],
        scratch=[pltpu.VMEM((rows, length + 2 * HALO), BF)],
        specs=[SMEM] + [None] * 4,
    )
    tied = lax.optimization_barrier((list(cut), all_hidden))
    cut, all_hidden = tied
    all_err = exchange_chan(cut)

    block_flops = 2 * blocks * 5 * channels * channels * width
    kept_shape = shaped((blocks, channels, width), BF)
    forward_outs = kernel_call(
        functools.partial(forward_kernel, pieces, blocks),
        [shaped((rows, own), BF)] * pieces + [kept_shape] * 5,
        [idx] + all_hidden + [plain, sample_id, silence_row],
        scratch=[
            pltpu.VMEM((channels, width), BF),
            pltpu.VMEM((3 * channels, width), BF),
            pltpu.VMEM((2 * channels, width), BF),
            pltpu.VMEM((channels, width), F32),
        ],
        flops=block_flops,
        specs=[SMEM] + [None] * (pieces + 3),
    )
    kept = list(forward_outs[pieces:])
    activation_parts = exchange_chan(list(forward_outs[:pieces]))

    backward_outs = kernel_call(
        functools.partial(backward_kernel, pieces, blocks),
        [shaped((rows, width), BF)] * pieces
        + [shaped((blocks * rows, packed_width), BF)] * pieces,
        [idx] + all_err + [dil_t, point_t, sample_id] + kept,
        scratch=[
            pltpu.VMEM((channels, width), BF),
            pltpu.VMEM((3 * channels, width), BF),
            pltpu.VMEM((channels, packed_width), BF),
        ],
        flops=2 * block_flops,
        specs=[SMEM] + [None] * (pieces + 8),
    )
    all_low = exchange_chan(list(backward_outs[:pieces]))
    block_grads = list(backward_outs[pieces:])

    total_rows = taps * rows
    split = total_rows % (32 * peers) == 0
    first = total_rows // peers // (2 if split else 1)
    near_shape = shaped((first, in_channels), BF)
    sums_width = in_channels + max(LANES, rows)
    back_outs = kernel_call(
        functools.partial(up_back_kernel, pieces, peers, split),
        [shaped((1, sums_width), F32)]
        + [shaped((in_rows, frames), BF)] * pieces
        + [near_shape] * half
        + [shaped((half, first, in_channels), BF)]
        + [shaped((2, first, in_channels), BF)] * (half if split else 0),
        [idx] + all_low + [up_w, upsample_direction, acted, frame_id, order],
        scratch=[
            pltpu.VMEM((rows, 8 * count), BF),
            pltpu.VMEM((8 * rows, count), BF),
            pltpu.VMEM((total_rows, frames), BF),
            pltpu.VMEM((in_channels, frames), BF),
            pltpu.VMEM((total_rows, in_channels), BF),
        ],
        flops=4 * taps * rows * in_channels * frames,
        specs=[SMEM] + [None] * (pieces + 5),
    )
    sums = back_outs[0]
    input_terms = list(back_outs[1 : 1 + pieces])
    near = list(back_outs[1 + pieces : 1 + pieces + half])
    far = back_outs[1 + pieces + half]
    duo = list(back_outs[2 + pieces + half :])

    far_got = swap(far, "tm", 1)
    if split:
        duo_got = [swap(duo[h], "tm", 2 * h) for h in range(1, half)]
        pair = add_low(duo[0], *duo_got)
        pair_high = swap(pair[1], "tm", 1)
        duo_own = add_low(pair[0], pair_high)
    near = [add_low(near[h], far_got[h]) for h in range(half)]
    near_got = [swap(near[h], "tm", 2 * h) for h in range(1, half)]
    near_own = add_low(near[0], *near_got)
    firsts = [near_own] + [swap(near_own, "tm", 2 * h) for h in range(1, half)]
    others = swap(jnp.stack(firsts), "tm", 1)
    duo_all = []
    if split:
        both = jnp.stack([duo_own, swap(duo_own, "tm", 1)])
        duo_all = [both] + [swap(both, "tm", 2 * h) for h in range(1, half)]
    inner_sum = lax.psum(sums[:, :in_channels], ("tm", "chan"))
    bias_sum = lax.psum(sums[:, in_channels:], "tm")

    input_total = scatter_chan(input_terms)
    (input_grad,) = kernel_call(
        input_kernel,
        [shaped((in_rows, frames), BF)],
        [input_total, spectrogram_input],
    )

    block_sum = scatter_chan(block_grads)
    size = -(-(blocks * rows) // (16 * half)) * 16
    block_sum = jnp.pad(block_sum, ((0, half * size - blocks * rows), (0, 0)))
    block_sum = block_sum.reshape(half, size, packed_width)
    cuts = [
        lax.dynamic_index_in_dim(block_sum, (tm >> 1) ^ h, keepdims=False) for h in range(half)
    ]
    part = add_low(cuts[0], *[swap(cuts[h], "tm", 2 * h) for h in range(1, half)])
    part = add_low(part, swap(part, "tm", 1))
    final_parts = [part] + [swap(part, "tm", 2 * h) for h in range(1, half)]
    block_outs = kernel_call(
        functools.partial(block_final_kernel, half),
        [
            shaped(dilated_direction.shape, F32),
            shaped(dilated_magnitude.shape, F32),
            shaped(dilated_bias.shape, F32),
            shaped(pointwise_direction.shape, F32),
            shaped(pointwise_magnitude.shape, F32),
            shaped(block_output_bias.shape, F32),
            shaped(shortcut_direction.shape, F32),
            shaped(shortcut_magnitude.shape, F32),
        ],
        [idx]
        + final_parts
        + [
            dilated_direction,
            dilated_magnitude,
            pointwise_direction,
            pointwise_magnitude,
            shortcut_direction,
            shortcut_magnitude,
        ],
        scratch=[pltpu.VMEM((half * size, packed_width), BF)],
        specs=[SMEM] + [None] * (half + 6),
    )
    dil_v_grad, dil_g_grad, dil_b_grad, mix_v_grad, mix_g_grad, out_b_grad = block_outs[:6]
    skip_v_grad, skip_g_grad = block_outs[6:]

    up_v_grad, up_g_grad = kernel_call(
        functools.partial(up_final_kernel, peers, split),
        [shaped(upsample_direction.shape, F32), shaped((1, in_channels), F32)],
        [idx] + firsts + [others] + duo_all + [upsample_direction, up_sq, up_g, inner_sum],
        scratch=[pltpu.VMEM((total_rows, in_channels), BF)],
        specs=[SMEM] + [None] * (half + 1 + len(duo_all) + 4),
    )
    (activation,) = kernel_call(
        functools.partial(join_kernel, pieces),
        [shaped((rows, length), BF)],
        [idx] + activation_parts,
        specs=[SMEM] + [None] * pieces,
    )
    return (
        activation,
        input_grad,
        up_v_grad,
        up_g_grad.reshape(in_channels),
        bias_sum[0, :rows],
        dil_v_grad,
        dil_g_grad,
        dil_b_grad,
        mix_v_grad,
        mix_g_grad,
        out_b_grad,
        skip_v_grad,
        skip_g_grad,
    )


def solution(mesh):
    placed = (
        P("chan", "tm"),
        P(None, "chan", None),
        P(),
        P("chan"),
        P(None, None, "chan", None),
        P(None, "chan"),
        P(None, "chan"),
        P(None, "chan", None),
        P(None, "chan"),
        P(None, "chan"),
        P(None, "chan", None),
        P(None, "chan"),
        P("chan", "tm"),
        P("tm"),
        P(),
    )
    return jax.shard_map(
        local,
        mesh=mesh,
        in_specs=placed,
        out_specs=(
            P("chan", "tm"),
            P("chan", "tm"),
            P(None, "chan", None),
            P(),
            P("chan"),
            P(None, None, "chan", None),
            P(None, "chan"),
            P(None, "chan"),
            P(None, "chan", None),
            P(None, "chan"),
            P(None, "chan"),
            P(None, "chan", None),
            P(None, "chan"),
        ),
        check_vma=False,
    )
```

time: 868 us -> 320 us (0.37)
  waiting for transfers between devices: 487 us -> 75.2 us
  matrix products: 165 us -> 0 us
  Pallas kernels: 0 us -> 103 us
  local copies, waits for them, and re-layouts: 80.9 us -> 10.8 us
  blocking collectives: 12.8 us -> 67.2 us
  other arithmetic: 51.7 us -> 3.12 us
  between operations: 16 us -> 1.38 us
  starting transfers between devices: 48.2 us -> 58.3 us
    reduce_scatter x6 -> x0, waiting for transfers between devices: 214 us -> none  [narrow(): lax.psum_scatter(values.astype(jnp.bfloat16), 'chan', scatter_dimension=0...]
    all_gather x7 -> x0, waiting for transfers between devices: 179 us -> none  [widen(): return lax.all_gather(values, 'chan', axis=0, tiled=True)]
    dot_general x48 -> x0, matrix products: 165 us -> none  [matrix_product(): jnp.einsum(form, left_op, right_op, preferred_element_type=jnp.float32)]
    pallas_call x0 -> x11, Pallas kernels: none -> 103 us  [kernel_call(): pl.pallas_call(body, out_shape=tuple(outs), in_specs=in_specs, out_specs=...]
    psum x1 -> x0, waiting for transfers between devices: 79.6 us -> none  [time_total(): return lax.psum(values.astype(jnp.bfloat16), 'tm').astype(jnp.float32)]
    ppermute x16 -> x54, waiting for transfers between devices: 13.7 us -> 75.2 us  [the longest x50 70.7 us: swap(): return lax.ppermute(values, axis, [(k, k ^ bit) for k in range(count)])]
    psum x2 -> x3, blocking collectives: 12.8 us -> 67.2 us  [the longest x1 38.4 us: local(): inner_sum = lax.psum(sums[:, :in_channels], ('tm', 'chan'))]
    concatenate x9 -> x1, local copies, waits for them, and re-layouts: 30.6 us -> 0.01 us  [local(): jnp.concatenate([lax.ppermute(spectrogram_input[:, frames - LANES:], 'tm'...]
  transfers between devices with their start and end apart: 31 -> 54, of which waited for: 19 -> 16; matrix products, arithmetic and copies ran while one was open for 20% -> 2% of each run, Pallas kernels for 0% -> 30%
where the time goes in v1:
time: 320 us; the launch traced here: 319 us
  Pallas kernels  103 us (32%)
  waiting for transfers between devices  75.2 us (24%)
  blocking collectives  67.2 us (21%)
  starting transfers between devices  58.3 us (18%)
  local copies, waits for them, and re-layouts  10.8 us (3%)
    pallas_call x11, Pallas kernels, kernel_call(): pl.pallas_call(body, out_shape=tuple(outs), in_specs=in_specs, out_specs=...  103 us
    ppermute x50, waiting for transfers between devices, swap(): return lax.ppermute(values, axis, [(k, k ^ bit) for k in range(count)])  70.7 us
    ppermute x50, starting transfers between devices, swap(): return lax.ppermute(values, axis, [(k, k ^ bit) for k in range(count)])  48.9 us
    psum x1, blocking collectives, local(): inner_sum = lax.psum(sums[:, :in_channels], ('tm', 'chan'))  38.4 us
    psum x1, blocking collectives, local(): bias_sum = lax.psum(sums[:, in_channels:], 'tm')  21 us
    psum x1, blocking collectives, local(): up_sq = lax.psum(up_sq, 'chan')  7.79 us
    unnamed x99, local copies, waits for them, and re-layouts  7.28 us
  transfers between devices with their start and end apart: 54, of which 16 were waited for; matrix products, arithmetic and copies ran while one was open for 2% of the time, Pallas kernels for 30%

profile of v1, /device:TPU:0, one launch (start us, length us, event | category | flops | bytes accessed | tf_op | source)
XLA Modules:
  0.0 319.5 jit_solution(1636890785081421876)
XLA Ops:
  0.7 5.0 %shard_map.246 = (f32[1,512]{1,0:T(1,128)}, bf16[192,1408]{1,0:T(8,128)(2,1)}, bf16[1024,1024]{1,0:T(8,128)(2,1)}, bf16[64,128]{1,0:T(8,128)(2,1)}, bf16[64,128]{1,0:T(8,128)(2,1)}) custom-call(f32[16,64,512]{2,1,0:T(8,128)} %refs_9_.2, f32[3,3,64,256]{3,2,1,0:T(8,128)} %refs_4_.1, f32[3,64]{1,0:T(4,128)} %refs_5_.3, f32[3,64]{1,0:T(4,128)} %dil_b.1, ...), custom_call_target="tpu_custom_call" | custom-call | bytes 6838016 | tf_op jit(solution)/shard_map/pallas_call | solution.py:70
  8.6 3.4 %collective-permute-start.5 = (bf16[128,128]{1,0:T(8,128)(2,1)S(1)}, bf16[128,128]{1,0:T(8,128)(2,1)S(1)}, u32[]{:S(2)}, u32[]{:S(2)}) collective-permute-start(bf16[128,128]{1,0:T(8,128)(2,1)S(1)} %get-tuple-element.154), channel_id=1, source_target_pairs={{0,4},{4,8},{8,12},{12,16},{16,20},{20,24},{24,28},{1,5},{5,9},{9,... | collective-permute-start | bytes 98312 | tf_op jit(solution)/shard_map/ppermute | solution.py:619
  14.0 4.5 %collective-permute-done.6 = bf16[128,128]{1,0:T(8,128)(2,1)S(1)} collective-permute-done((bf16[128,128]{1,0:T(8,128)(2,1)S(1)}, bf16[128,128]{1,0:T(8,128)(2,1)S(1)}, u32[]{:S(2)}, u32[]{:S(2)}) %collective-permute-start.6) | collective-permute-done | bytes 32800 | tf_op jit(solution)/shard_map/ppermute | solution.py:620
  20.0 7.4 %collective-permute-done.3.refs_2_ = bf16[128,1024]{1,0:T(8,128)(2,1)S(1)} collective-permute-done((bf16[128,1024]{1,0:T(8,128)(2,1)S(1)}, bf16[128,1024]{1,0:T(8,128)(2,1)S(1)}, u32[]{:S(2)}, u32[]{:S(2)}) %collective-permute-start.3) | collective-permute-done | bytes 262176 | tf_op jit(solution)/shard_map/ppermute | solution.py:21
  29.3 7.8 %psum.21.refs_9_.refs_10_ = f32[1,512]{1,0:T(1,128)} all-reduce(f32[1,512]{1,0:T(1,128)} %get-tuple-element.86), channel_id=1, replica_groups=mesh['tm'=8,'chan'=4] {'chan'}, use_global_device_ids=true, to_apply=%region_0.1 | all-reduce | flops 512 | bytes 4096 | tf_op jit(solution)/shard_map/psum | solution.py:661
  38.3 3.4 %collective-permute-start = (bf16[64,128]{1,0:T(8,128)(2,1)}, bf16[64,128]{1,0:T(8,128)(2,1)S(1)}, u32[]{:S(2)}, u32[]{:S(2)}) collective-permute-start(bf16[64,128]{1,0:T(8,128)(2,1)} %get-tuple-element.80), channel_id=1, source_target_pairs={{0,4},{4,8},{8,12},{12,16},{16,20},{20,24},{24,28},{1,5},{5,9},{9,... | collective-permute-start | bytes 49160 | tf_op jit(solution)/shard_map/ppermute | solution.py:663
  43.8 10.0 %shard_map.248 = (bf16[64,2304]{1,0:T(8,128)(2,1)}, bf16[64,2304]{1,0:T(8,128)(2,1)}, bf16[64,2304]{1,0:T(8,128)(2,1)}, bf16[64,2304]{1,0:T(8,128)(2,1)}, bf16[5...) custom-call(s32[2]{0:T(128)} %pad_add_fusion.idx, bf16[128,1024]{1,0:T(8,128)(2,1)} %refs_1_.1, ...), custom_call_target="tpu_custom_call" | custom-call | flops 1207959552 | bytes 8791304 | tf_op jit(solution)/shard_map/pallas_call | solution.py:70
  59.5 4.6 %collective-permute-done.11.refs_2_ = bf16[64,2304]{1,0:T(8,128)(2,1)S(1)} collective-permute-done((bf16[64,2304]{1,0:T(8,128)(2,1)}, bf16[64,2304]{1,0:T(8,128)(2,1)S(1)}, u32[]{:S(2)}, u32[]{:S(2)}) %collective-permute-start.11) | collective-permute-done | bytes 294944 | tf_op jit(solution)/shard_map/ppermute | solution.py:21
  64.0 5.4 %collective-permute-done.12.refs_3_ = bf16[64,2304]{1,0:T(8,128)(2,1)S(1)} collective-permute-done((bf16[64,2304]{1,0:T(8,128)(2,1)}, bf16[64,2304]{1,0:T(8,128)(2,1)S(1)}, u32[]{:S(2)}, u32[]{:S(2)}) %collective-permute-start.12) | collective-permute-done | bytes 294944 | tf_op jit(solution)/shard_map/ppermute | solution.py:21
  72.9 3.7 %shard_map.249 = (bf16[3,256,1408]{2,1,0:T(8,128)(2,1)}, bf16[3,256,768]{2,1,0:T(8,128)(2,1)}, bf16[3,256,512]{2,1,0:T(8,128)(2,1)}) custom-call(s32[2]{0:T(128)} %pad_add_fusion.idx, bf16[192,1408]{1,0:T(8,128)(2,1)} %get-tuple-element.96.refs_0_, bf16[192,1408]{1,0:T(8,128)(2,1)} %copy-done.5, bf16[192,1408]{1,0:T(8,128)(2,1)} %copy-done.4, ...), custom_call_target="tpu_custom_call" | custom-call | bytes 6291464 | tf_op jit(solution)/shard_map/pallas_call | solution.py:70
  76.6 31.3 %shard_map.250 = (bf16[64,2048]{1,0:T(8,128)(2,1)}, bf16[64,2048]{1,0:T(8,128)(2,1)}, bf16[64,2048]{1,0:T(8,128)(2,1)}, bf16[64,2048]{1,0:T(8,128)(2,1)}, bf16[3...) custom-call(s32[2]{0:T(128)} %pad_add_fusion.idx, ...), custom_call_target="tpu_custom_call" | custom-call | flops 4529848320 | bytes 22127624 | tf_op jit(solution)/shard_map/pallas_call | solution.py:70
  109.5 27.2 %shard_map.252 = (bf16[64,2304]{1,0:T(8,128)(2,1)}, bf16[64,2304]{1,0:T(8,128)(2,1)}, bf16[64,2304]{1,0:T(8,128)(2,1)}, bf16[64,2304]{1,0:T(8,128)(2,1)}, bf16[1...) custom-call(s32[2]{0:T(128)} %pad_add_fusion.idx, ...), custom_call_target="tpu_custom_call" | custom-call | flops 9059696640 | bytes 24192008 | tf_op jit(solution)/shard_map/pallas_call | solution.py:70
  140.4 18.4 %collective-permute-done.17.refs_2_ = bf16[64,2048]{1,0:T(8,128)(2,1)S(1)} collective-permute-done((bf16[64,2048]{1,0:T(8,128)(2,1)S(1)}, bf16[64,2048]{1,0:T(8,128)(2,1)S(1)}, u32[]{:S(2)}, u32[]{:S(2)}) %collective-permute-start.17) | collective-permute-done | bytes 262176 | tf_op jit(solution)/shard_map/ppermute | solution.py:21
  158.8 4.7 %collective-permute-done.18.refs_3_ = bf16[64,2048]{1,0:T(8,128)(2,1)S(1)} collective-permute-done((bf16[64,2048]{1,0:T(8,128)(2,1)S(1)}, bf16[64,2048]{1,0:T(8,128)(2,1)S(1)}, u32[]{:S(2)}, u32[]{:S(2)}) %collective-permute-start.18) | collective-permute-done | bytes 262176 | tf_op jit(solution)/shard_map/ppermute | solution.py:21
  167.4 12.7 %shard_map.253 = (f32[1,640]{1,0:T(1,128)}, bf16[128,1024]{1,0:T(8,128)(2,1)}, bf16[128,1024]{1,0:T(8,128)(2,1)}, bf16[128,1024]{1,0:T(8,128)(2,1)}, bf16[128,10...) custom-call(s32[2]{0:T(128)} %pad_add_fusion.idx, ...), custom_call_target="tpu_custom_call" | custom-call | flops 2147483648 | bytes 9575944 | tf_op jit(solution)/shard_map/pallas_call | solution.py:70
  180.1 3.7 %collective-permute-start.36 = (bf16[2,64,512]{2,1,0:T(8,128)(2,1)}, bf16[2,64,512]{2,1,0:T(8,128)(2,1)S(1)}, u32[]{:S(2)}, u32[]{:S(2)}) collective-permute-start(bf16[2,64,512]{2,1,0:T(8,128)(2,1)} %get-tuple-element.129), channel_id=1, source_target_pairs={{0,8},{4,12},{8,0},{12,4},{16,24},{20,28},{24,16},{28,20},{1,9},{5... | collective-permute-start | bytes 393224 | tf_op jit(solution)/shard_map/ppermute | solution.py:21
  187.0 21.0 %psum.23 = f32[1,128]{1,0:T(1,128)S(1)} all-reduce(f32[1,128]{1,0:T(1,128)S(1)} %slice.42), channel_id=1, replica_groups=mesh['tm'=8,'chan'=4] {'tm'}, use_global_device_ids=true, to_apply=%region_2.3 | all-reduce | flops 128 | bytes 1024 | tf_op jit(solution)/shard_map/psum | solution.py:789
  209.2 38.4 %psum.22.refs_12_ = f32[1,512]{1,0:T(1,128)} all-reduce(f32[1,512]{1,0:T(1,128)S(1)} %slice.41), channel_id=1, replica_groups=mesh['tm'=8,'chan'=4] {'tm','chan'}, use_global_device_ids=true, to_apply=%region_1.2 | all-reduce | flops 512 | bytes 4096 | tf_op jit(solution)/shard_map/psum | solution.py:788
  252.0 4.7 %collective-permute-done.39 = bf16[64,512]{1,0:T(8,128)(2,1)S(1)} collective-permute-done((bf16[64,512]{1,0:T(8,128)(2,1)S(1)}, bf16[64,512]{1,0:T(8,128)(2,1)S(1)}, u32[]{:S(2)}, u32[]{:S(2)}) %collective-permute-start.39) | collective-permute-done | bytes 65568 | tf_op jit(solution)/shard_map/ppermute | solution.py:21
  262.9 7.4 %collective-permute-done.46 = bf16[192,1408]{1,0:T(8,128)(2,1)S(1)} collective-permute-done((bf16[192,1408]{1,0:T(8,128)(2,1)S(1)}, bf16[192,1408]{1,0:T(8,128)(2,1)S(1)}, u32[]{:S(2)}, u32[]{:S(2)}) %collective-permute-start.46) | collective-permute-done | bytes 540704 | tf_op jit(solution)/shard_map/ppermute | solution.py:21
  281.2 4.9 %collective-permute-done.48 = bf16[48,1408]{1,0:T(8,128)(2,1)S(1)} collective-permute-done((bf16[48,1408]{1,0:T(8,128)(2,1)S(1)}, bf16[48,1408]{1,0:T(8,128)(2,1)S(1)}, u32[]{:S(2)}, u32[]{:S(2)}) %collective-permute-start.48) | collective-permute-done | bytes 135200 | tf_op jit(solution)/shard_map/ppermute | solution.py:21
  298.9 6.3 %collective-permute-done.42.refs_7_ = bf16[2,64,512]{2,1,0:T(8,128)(2,1)S(1)} collective-permute-done((bf16[2,64,512]{2,1,0:T(8,128)(2,1)S(1)}, bf16[2,64,512]{2,1,0:T(8,128)(2,1)S(1)}, u32[]{:S(2)}, u32[]{:S(2)}) %collective-permute-start.42) | collective-permute-done | bytes 131104 | tf_op jit(solution)/shard_map/ppermute | solution.py:21
  310.1 3.6 %shard_map.255 = (f32[16,64,512]{2,1,0:T(8,128)}, f32[1,512]{1,0:T(1,128)}) custom-call(s32[2]{0:T(128)} %pad_add_fusion.idx, bf16[64,512]{1,0:T(8,128)(2,1)} %copy-done.1, bf16[64,512]{1,0:T(8,128)(2,1)} %copy-done.18, bf16[64,512]{1,0:T(8,128)(2,1)} %copy-done.19, bf16[64,512]{1,0:T(8,128)(2,1)} %copy-done.20, bf16[4,64,512]{2,1,0:T(8,128)(2,1)} %copy-done.15, ...), custom_call_target="tpu_custom_call" | custom-call | bytes 5251080 | tf_op jit(solution)/shard_map/pallas_call | solution.py:70
  316.4 3.0 shard_map.256
  (223 shorter events, 75.7 us)
Async XLA Ops:
  5.7 22.5 %collective-permute-start.14 = (bf16[192,1408]{1,0:T(8,128)(2,1)}, bf16[192,1408]{1,0:T(8,128)(2,1)S(1)}, u32[]{:S(2)}, u32[]{:S(2)}) collective-permute-start(bf16[192,1408]{1,0:T(8,128)(2,1)} %get-tuple-element.96.refs_0_), channel_id=1, source_target_pairs={{0,2},{1,3},{2,0},{3,1},{4,6},{5,7},{6,4},{7,5},{8,10},{9,11},{10,... | collective-permute-start | bytes 1622024 | tf_op jit(solution)/shard_map/ppermute | solution.py:21
  12.0 15.4 %collective-permute-start.3 = (bf16[128,1024]{1,0:T(8,128)(2,1)S(1)}, bf16[128,1024]{1,0:T(8,128)(2,1)S(1)}, u32[]{:S(2)}, u32[]{:S(2)}) collective-permute-start(bf16[128,1024]{1,0:T(8,128)(2,1)S(1)} %copy-done), channel_id=1, source_target_pairs={{0,2},{1,3},{2,0},{3,1},{4,6},{5,7},{6,4},{7,5},{8,10},{9,11},{10,... | collective-permute-start | bytes 786440 | tf_op jit(solution)/shard_map/ppermute | solution.py:21
  20.0 21.7 %collective-permute-start.2 = (bf16[128,1024]{1,0:T(8,128)(2,1)S(1)}, bf16[128,1024]{1,0:T(8,128)(2,1)S(1)}, u32[]{:S(2)}, u32[]{:S(2)}) collective-permute-start(bf16[128,1024]{1,0:T(8,128)(2,1)S(1)} %copy-done), channel_id=1, source_target_pairs={{0,1},{1,0},{2,3},{3,2},{4,5},{5,4},{6,7},{7,6},{8,9},{9,8},{10,11... | collective-permute-start | bytes 786440 | tf_op jit(solution)/shard_map/ppermute | solution.py:21
  27.4 15.7 %collective-permute-start.4 = (bf16[128,1024]{1,0:T(8,128)(2,1)S(1)}, bf16[128,1024]{1,0:T(8,128)(2,1)S(1)}, u32[]{:S(2)}, u32[]{:S(2)}) collective-permute-start(bf16[128,1024]{1,0:T(8,128)(2,1)S(1)} %collective-permute-done.3.refs_2_), channel_id=1, source_target_pairs={{0,1},{1,0},{2,3},{3,2},{4,5},{5,4},{6,7},{7,6},{8,9},{9,8},{10,11... | collective-permute-start | bytes 786440 | tf_op jit(solution)/shard_map/ppermute | solution.py:21
  27.4 43.9 %collective-permute-start.13 = (bf16[192,1408]{1,0:T(8,128)(2,1)}, bf16[192,1408]{1,0:T(8,128)(2,1)S(1)}, u32[]{:S(2)}, u32[]{:S(2)}) collective-permute-start(bf16[192,1408]{1,0:T(8,128)(2,1)} %get-tuple-element.96.refs_0_), channel_id=1, source_target_pairs={{0,1},{1,0},{2,3},{3,2},{4,5},{5,4},{6,7},{7,6},{8,9},{9,8},{10,11... | collective-permute-start | bytes 1622024 | tf_op jit(solution)/shard_map/ppermute | solution.py:21
  28.1 43.2 %collective-permute-start.15 = (bf16[192,1408]{1,0:T(8,128)(2,1)S(1)}, bf16[192,1408]{1,0:T(8,128)(2,1)S(1)}, u32[]{:S(2)}, u32[]{:S(2)}) collective-permute-start(bf16[192,1408]{1,0:T(8,128)(2,1)S(1)} %collective-permute-done.14.refs_2_), channel_id=1, source_target_pairs={{0,1},{1,0},{2,3},{3,2},{4,5},{5,4},{6,7},{7,6},{8,9},{9,8},{10,11... | collective-permute-start | bytes 1622024 | tf_op jit(solution)/shard_map/ppermute | solution.py:21
  38.3 15.6 %collective-permute-start = (bf16[64,128]{1,0:T(8,128)(2,1)}, bf16[64,128]{1,0:T(8,128)(2,1)S(1)}, u32[]{:S(2)}, u32[]{:S(2)}) collective-permute-start(bf16[64,128]{1,0:T(8,128)(2,1)} %get-tuple-element.80), channel_id=1, source_target_pairs={{0,4},{4,8},{8,12},{12,16},{16,20},{20,24},{24,28},{1,5},{5,9},{9,... | collective-permute-start | bytes 49160 | tf_op jit(solution)/shard_map/ppermute | solution.py:663
  69.4 39.1 %collective-permute-start.19 = (bf16[64,2304]{1,0:T(8,128)(2,1)}, bf16[64,2304]{1,0:T(8,128)(2,1)S(1)}, u32[]{:S(2)}, u32[]{:S(2)}) collective-permute-start(bf16[64,2304]{1,0:T(8,128)(2,1)} %get-tuple-element.103), channel_id=1, source_target_pairs={{0,1},{1,0},{2,3},{3,2},{4,5},{5,4},{6,7},{7,6},{8,9},{9,8},{10,11... | collective-permute-start | bytes 884744 | tf_op jit(solution)/shard_map/ppermute | solution.py:21
  69.7 38.9 %collective-permute-start.20 = (bf16[64,2304]{1,0:T(8,128)(2,1)}, bf16[64,2304]{1,0:T(8,128)(2,1)S(1)}, u32[]{:S(2)}, u32[]{:S(2)}) collective-permute-start(bf16[64,2304]{1,0:T(8,128)(2,1)} %get-tuple-element.104), channel_id=1, source_target_pairs={{0,2},{1,3},{2,0},{3,1},{4,6},{5,7},{6,4},{7,5},{8,10},{9,11},{10,... | collective-permute-start | bytes 884744 | tf_op jit(solution)/shard_map/ppermute | solution.py:21
  70.2 38.3 %collective-permute-start.21 = (bf16[64,2304]{1,0:T(8,128)(2,1)}, bf16[64,2304]{1,0:T(8,128)(2,1)S(1)}, u32[]{:S(2)}, u32[]{:S(2)}) collective-permute-start(bf16[64,2304]{1,0:T(8,128)(2,1)} %get-tuple-element.105), channel_id=1, source_target_pairs={{0,3},{1,2},{2,1},{3,0},{4,7},{5,6},{6,5},{7,4},{8,11},{9,10},{10,... | collective-permute-start | bytes 884744 | tf_op jit(solution)/shard_map/ppermute | solution.py:21
  107.9 31.2 %collective-permute-start.16 = (bf16[64,2048]{1,0:T(8,128)(2,1)}, bf16[64,2048]{1,0:T(8,128)(2,1)S(1)}, u32[]{:S(2)}, u32[]{:S(2)}) collective-permute-start(bf16[64,2048]{1,0:T(8,128)(2,1)} %get-tuple-element.99), channel_id=1, source_target_pairs={{0,1},{1,0},{2,3},{3,2},{4,5},{5,4},{6,7},{7,6},{8,9},{9,8},{10,11... | collective-permute-start | bytes 786440 | tf_op jit(solution)/shard_map/ppermute | solution.py:21
  136.7 29.7 %collective-permute-start.22 = (bf16[64,2304]{1,0:T(8,128)(2,1)}, bf16[64,2304]{1,0:T(8,128)(2,1)S(1)}, u32[]{:S(2)}, u32[]{:S(2)}) collective-permute-start(bf16[64,2304]{1,0:T(8,128)(2,1)} %get-tuple-element.114), channel_id=1, source_target_pairs={{0,1},{1,0},{2,3},{3,2},{4,5},{5,4},{6,7},{7,6},{8,9},{9,8},{10,11... | collective-permute-start | bytes 884744 | tf_op jit(solution)/shard_map/ppermute | solution.py:21
  136.8 29.7 %collective-permute-start.23 = (bf16[64,2304]{1,0:T(8,128)(2,1)}, bf16[64,2304]{1,0:T(8,128)(2,1)S(1)}, u32[]{:S(2)}, u32[]{:S(2)}) collective-permute-start(bf16[64,2304]{1,0:T(8,128)(2,1)} %get-tuple-element.115), channel_id=1, source_target_pairs={{0,2},{1,3},{2,0},{3,1},{4,6},{5,7},{6,4},{7,5},{8,10},{9,11},{10,... | collective-permute-start | bytes 884744 | tf_op jit(solution)/shard_map/ppermute | solution.py:21
  137.3 29.1 %collective-permute-start.24 = (bf16[64,2304]{1,0:T(8,128)(2,1)}, bf16[64,2304]{1,0:T(8,128)(2,1)S(1)}, u32[]{:S(2)}, u32[]{:S(2)}) collective-permute-start(bf16[64,2304]{1,0:T(8,128)(2,1)} %get-tuple-element.116), channel_id=1, source_target_pairs={{0,3},{1,2},{2,1},{3,0},{4,7},{5,6},{6,5},{7,4},{8,11},{9,10},{10,... | collective-permute-start | bytes 884744 | tf_op jit(solution)/shard_map/ppermute | solution.py:21
  138.6 20.2 %collective-permute-start.17 = (bf16[64,2048]{1,0:T(8,128)(2,1)S(1)}, bf16[64,2048]{1,0:T(8,128)(2,1)S(1)}, u32[]{:S(2)}, u32[]{:S(2)}) collective-permute-start(bf16[64,2048]{1,0:T(8,128)(2,1)S(1)} %copy-done.48), channel_id=1, source_target_pairs={{0,2},{1,3},{2,0},{3,1},{4,6},{5,7},{6,4},{7,5},{8,10},{9,11},{10,... | collective-permute-start | bytes 786440 | tf_op jit(solution)/shard_map/ppermute | solution.py:21
  139.1 24.3 %collective-permute-start.18 = (bf16[64,2048]{1,0:T(8,128)(2,1)S(1)}, bf16[64,2048]{1,0:T(8,128)(2,1)S(1)}, u32[]{:S(2)}, u32[]{:S(2)}) collective-permute-start(bf16[64,2048]{1,0:T(8,128)(2,1)S(1)} %copy-done.47), channel_id=1, source_target_pairs={{0,3},{1,2},{2,1},{3,0},{4,7},{5,6},{6,5},{7,4},{8,11},{9,10},{10,... | collective-permute-start | bytes 786440 | tf_op jit(solution)/shard_map/ppermute | solution.py:21
  158.8 93.0 %collective-permute-start.45 = (bf16[192,1408]{1,0:T(8,128)(2,1)}, bf16[192,1408]{1,0:T(8,128)(2,1)S(1)}, u32[]{:S(2)}, u32[]{:S(2)}) collective-permute-start(bf16[192,1408]{1,0:T(8,128)(2,1)} %get-tuple-element.138), channel_id=1, source_target_pairs={{0,1},{1,0},{2,3},{3,2},{4,5},{5,4},{6,7},{7,6},{8,9},{9,8},{10,11... | collective-permute-start | bytes 1622024 | tf_op jit(solution)/shard_map/ppermute | solution.py:21
  163.4 97.7 %collective-permute-start.44 = (bf16[192,1408]{1,0:T(8,128)(2,1)}, bf16[192,1408]{1,0:T(8,128)(2,1)S(1)}, u32[]{:S(2)}, u32[]{:S(2)}) collective-permute-start(bf16[192,1408]{1,0:T(8,128)(2,1)} %get-tuple-element.136), channel_id=1, source_target_pairs={{0,1},{1,0},{2,3},{3,2},{4,5},{5,4},{6,7},{7,6},{8,9},{9,8},{10,11... | collective-permute-start | bytes 1622024 | tf_op jit(solution)/shard_map/ppermute | solution.py:21
  180.1 67.5 %collective-permute-start.36 = (bf16[2,64,512]{2,1,0:T(8,128)(2,1)}, bf16[2,64,512]{2,1,0:T(8,128)(2,1)S(1)}, u32[]{:S(2)}, u32[]{:S(2)}) collective-permute-start(bf16[2,64,512]{2,1,0:T(8,128)(2,1)} %get-tuple-element.129), channel_id=1, source_target_pairs={{0,8},{4,12},{8,0},{12,4},{16,24},{20,28},{24,16},{28,20},{1,9},{5... | collective-permute-start | bytes 393224 | tf_op jit(solution)/shard_map/ppermute | solution.py:21
  183.8 66.4 %collective-permute-start.37 = (bf16[2,64,512]{2,1,0:T(8,128)(2,1)}, bf16[2,64,512]{2,1,0:T(8,128)(2,1)S(1)}, u32[]{:S(2)}, u32[]{:S(2)}) collective-permute-start(bf16[2,64,512]{2,1,0:T(8,128)(2,1)} %get-tuple-element.130), channel_id=1, source_target_pairs={{0,16},{4,20},{8,24},{12,28},{16,0},{20,4},{24,8},{28,12},{1,17},{... | collective-permute-start | bytes 393224 | tf_op jit(solution)/shard_map/ppermute | solution.py:21
  186.4 63.8 %collective-permute-start.38 = (bf16[2,64,512]{2,1,0:T(8,128)(2,1)}, bf16[2,64,512]{2,1,0:T(8,128)(2,1)S(1)}, u32[]{:S(2)}, u32[]{:S(2)}) collective-permute-start(bf16[2,64,512]{2,1,0:T(8,128)(2,1)} %get-tuple-element.131), channel_id=1, source_target_pairs={{0,24},{4,28},{8,16},{12,20},{16,8},{20,12},{24,0},{28,4},{1,25},{... | collective-permute-start | bytes 393224 | tf_op jit(solution)/shard_map/ppermute | solution.py:21
  250.2 45.2 %collective-permute-start.25 = (bf16[128,1024]{1,0:T(8,128)(2,1)}, bf16[128,1024]{1,0:T(8,128)(2,1)S(1)}, u32[]{:S(2)}, u32[]{:S(2)}) collective-permute-start(bf16[128,1024]{1,0:T(8,128)(2,1)} %get-tuple-element.120), channel_id=1, source_target_pairs={{0,1},{1,0},{2,3},{3,2},{4,5},{5,4},{6,7},{7,6},{8,9},{9,8},{10,11... | collective-permute-start | bytes 786440 | tf_op jit(solution)/shard_map/ppermute | solution.py:21
  258.3 29.3 %collective-permute-start.40 = (bf16[64,512]{1,0:T(8,128)(2,1)S(1)}, bf16[64,512]{1,0:T(8,128)(2,1)S(1)}, u32[]{:S(2)}, u32[]{:S(2)}) collective-permute-start(bf16[64,512]{1,0:T(8,128)(2,1)S(1)} %fusion.3), channel_id=1, source_target_pairs={{0,4},{4,0},{8,12},{12,8},{16,20},{20,16},{24,28},{28,24},{1,5},{5... | collective-permute-start | bytes 196616 | tf_op jit(solution)/shard_map/ppermute | solution.py:21
  297.0 16.8 %collective-permute-start.51 = (bf16[48,1408]{1,0:T(8,128)(2,1)S(1)}, bf16[48,1408]{1,0:T(8,128)(2,1)S(1)}, u32[]{:S(2)}, u32[]{:S(2)}) collective-permute-start(bf16[48,1408]{1,0:T(8,128)(2,1)S(1)} %add_convert_fusion.6.refs_0_), channel_id=1, source_target_pairs={{0,8},{4,12},{8,0},{12,4},{16,24},{20,28},{24,16},{28,20},{1,9},{5... | collective-permute-start | bytes 405512 | tf_op jit(solution)/shard_map/ppermute | solution.py:21
  (79 other events, 856.3 us)

commit v2 on v1

v2 whole, which is shorter than its diff:
```python
import functools

import jax
import jax.numpy as jnp
from jax import lax
from jax.experimental import pallas as pl
from jax.experimental.pallas import tpu as pltpu
from jax.sharding import PartitionSpec as P

BF = jnp.bfloat16
F32 = jnp.float32
LANES = 128
HALO = 128
TAIL = 128
SUMS = 16
VMEM_LIMIT = 24 * 1024 * 1024


def swap(values, axis, bit):
    count = lax.axis_size(axis)
    return lax.ppermute(values, axis, [(k, k ^ bit) for k in range(count)])


def bits_of(count):
    bits = []
    bit = 1
    while bit < count:
        bits.append(bit)
        bit = 2 * bit
    return bits


def order_of(bits):
    order = [0]
    for bit in reversed(bits):
        order = order + [slot + bit for slot in order]
    return order


def gather_chan(own):
    held = {0: own}
    for bit in reversed(bits_of(lax.axis_size("chan"))):
        for slot in list(held):
            held[slot ^ bit] = swap(held[slot], "chan", bit)
    return [held[slot] for slot in range(len(held))]


def exchange_chan(pieces):
    return [pieces[0]] + [swap(pieces[s], "chan", s) for s in range(1, len(pieces))]


HBM = pl.BlockSpec(memory_space=pltpu.HBM)
ANY = pl.BlockSpec(memory_space=pl.ANY)
VMEM = pl.BlockSpec(memory_space=pltpu.VMEM)


def kernel_call(body, outs, args, specs, scratch=(), micros=1.0):
    held = []
    in_specs = []
    operands = []
    for arg, spec in zip(args, specs, strict=True):
        in_specs.append({"H": HBM, "F": HBM, "A": ANY, "G": ANY, "R": VMEM}[spec])
        if spec in "FG":
            held.append(pltpu.VMEM(arg.shape, arg.dtype))
        if spec == "R":
            arg = pltpu.with_memory_space_constraint(arg, pltpu.VMEM)
        if spec in "HF":
            arg = pltpu.with_memory_space_constraint(arg, pltpu.HBM)
        operands.append(arg)
    out_shape = []
    out_specs = []
    for shape, dtype, spec in outs:
        out_specs.append(HBM if spec == "H" else VMEM)
        spaced = {"R": pltpu.VMEM, "H": pltpu.HBM, "V": jax.ShapeDtypeStruct}[spec]
        out_shape.append(spaced(shape, dtype))
    fetched = len(held)

    def wrapped(*refs):
        refs = list(refs)
        if fetched:
            sems = refs.pop()
            targets = refs[-fetched:]
            refs = refs[:-fetched]
            sources = [number for number, spec in enumerate(specs) if spec in "FG"]
            fetch([(refs[n], target) for n, target in zip(sources, targets)], sems)
            for n, target in zip(sources, targets):
                refs[n] = target
        body((lax.axis_index("tm"), lax.axis_index("chan")), *refs)

    extra = held + ([pltpu.SemaphoreType.DMA((fetched,))] if fetched else [])
    return pl.pallas_call(
        wrapped,
        out_shape=tuple(out_shape),
        in_specs=in_specs,
        out_specs=tuple(out_specs),
        scratch_shapes=list(scratch) + extra,
        compiler_params=pltpu.CompilerParams(vmem_limit_bytes=VMEM_LIMIT),
        cost_estimate=pl.CostEstimate(
            flops=int(micros * 1.1e9), bytes_accessed=0, transcendentals=0
        ),
    )(*operands)


def fetch(pairs, sems):
    copies = [
        pltpu.make_async_copy(source, target, sems.at[number])
        for number, (source, target) in enumerate(pairs)
    ]
    for copy in copies:
        copy.start()
    for copy in copies:
        copy.wait()


def unit(values):
    th = jnp.tanh(0.5 * values)
    base = 0.6 + 0.4 * th
    return values * base, base + 0.2 * values * (1.0 - th * th)


def unit_act(values):
    return values * (0.6 + 0.4 * jnp.tanh(0.5 * values))


def dot(left, right):
    return lax.dot_general(left, right, (((1,), (0,)), ((), ())), preferred_element_type=F32)


def dot_rt(left, right):
    return lax.dot_general(left, right, (((1,), (1,)), ((), ())), preferred_element_type=F32)


def eye_mask(count):
    rows = lax.broadcasted_iota(jnp.int32, (count, count), 0)
    cols = lax.broadcasted_iota(jnp.int32, (count, count), 1)
    return rows == cols


def to_col(row, eye):
    return jnp.sum(jnp.where(eye, row, 0.0), axis=1, keepdims=True)


def to_row(col, eye):
    return jnp.sum(jnp.where(eye, col, 0.0), axis=0, keepdims=True)


def at(start, size, step):
    return pl.ds(pl.multiple_of(start, step), size)


def edge_kernel(idx, spectrogram, cot, sil, ahead, behind, front, back, sound, mask, sems):
    rows = spectrogram.shape[0]
    frames, count = spectrogram.shape[1], cot.shape[1]
    low, high = pl.ds(0, HALO), pl.ds(count - HALO, HALO)
    fetch(
        [
            (spectrogram.at[:, frames - LANES :], front),
            (spectrogram.at[:, :LANES], back),
            (cot.at[:, high], sound.at[0]),
            (cot.at[:, low], sound.at[1]),
            (sil.at[:, high], mask.at[0]),
            (sil.at[:, low], mask.at[1]),
        ],
        sems,
    )
    ahead[0:rows, :] = front[...]
    behind[0:rows, :] = back[...]
    ahead[rows:, :] = (sound[0].astype(F32) * mask[0].astype(F32)).astype(BF)
    behind[rows:, :] = (sound[1].astype(F32) * mask[1].astype(F32)).astype(BF)


def square_kernel(idx, up_v, up_sq):
    total = jnp.zeros((up_v.shape[1], up_v.shape[2]), F32)
    for k in range(up_v.shape[0]):
        rows = up_v[k]
        total = total + rows * rows
    up_sq[...] = jnp.sum(total, axis=0, keepdims=True)


def prep_kernel(
    idx, dil_v, dil_g, dil_b, mix_v, mix_g, out_b, skip_v, skip_g, packed, near, far, order,
    held, sem
):
    size = order.shape[0]
    source = lax.broadcasted_iota(jnp.int32, (size, size), 0)
    target = lax.broadcasted_iota(jnp.int32, (size, size), 1)
    hit = target == 8 * (source & (LANES - 1)) + (source >> 7)
    held[...] = jnp.where(hit, 1.0, 0.0).astype(BF)
    copy = pltpu.make_async_copy(held, order, sem)
    copy.start()
    local_out = dil_v.shape[2]
    eye = eye_mask(local_out)
    lane = lax.broadcasted_iota(jnp.int32, (local_out, TAIL), 1)
    width = dil_v.shape[3]
    for j in range(dil_v.shape[0]):
        rows = pl.ds(j * local_out, local_out)
        square = jnp.zeros((local_out, 1), F32)
        for k in range(3):
            v = dil_v[j, k]
            square = square + jnp.sum(v * v, axis=1, keepdims=True)
        norm = jnp.sqrt(square)
        gain = to_col(dil_g[j : j + 1, :], eye)
        for k in range(3):
            packed[rows, k * width : (k + 1) * width] = (gain * dil_v[j, k] / norm).astype(BF)
        for number, (vref, gref) in enumerate(((mix_v, mix_g), (skip_v, skip_g))):
            v = vref[j]
            norm = jnp.sqrt(jnp.sum(v * v, axis=1, keepdims=True))
            gain = to_col(gref[j : j + 1, :], eye)
            packed[rows, (3 + number) * width : (4 + number) * width] = (gain * v / norm).astype(BF)
        first = to_col(dil_b[j : j + 1, :], eye)
        second = to_col(out_b[j : j + 1, :], eye)
        high_one = first.astype(BF).astype(F32)
        high_two = second.astype(BF).astype(F32)
        tail = jnp.where(lane == 0, high_one, 0.0) + jnp.where(lane == 1, first - high_one, 0.0)
        tail = tail + jnp.where(lane == 2, high_two, 0.0)
        tail = tail + jnp.where(lane == 3, second - high_two, 0.0)
        packed[rows, 5 * width : 5 * width + TAIL] = tail.astype(BF)
    half = near.shape[0]
    for number, target in enumerate((near, far)):
        target[...] = packed[at(((idx[0] ^ number) & 1) * half, half, 16), :]
    copy.wait()


def cut_kernel(pieces, idx, cot, sil, low, high, *refs):
    outs, wide, sems = refs[:pieces], refs[pieces], refs[pieces + 1]
    count = cot.shape[1]
    own = count // pieces
    rows = cot.shape[0]
    wide[:, 0:HALO] = low[low.shape[0] - rows :, :]
    wide[:, HALO : HALO + count] = (cot[...].astype(F32) * sil[...].astype(F32)).astype(BF)
    wide[:, HALO + count :] = high[high.shape[0] - rows :, :]
    fetch(
        [
            (wide.at[:, at((idx[1] ^ s) * own, own + 2 * HALO, LANES)], outs[s])
            for s in range(pieces)
        ],
        sems,
    )


def weight_kernel(pieces, blocks, idx, *refs):
    *parts, plain, dil_t, point_t, sems = refs
    rows = parts[0].shape[0] // blocks
    part = rows // 2
    pairs = []
    for s in range(pieces):
        start = (idx[1] ^ s) * rows
        if s < 2:
            for j in range(blocks):
                source = parts[s].at[j * rows : (j + 1) * rows, :]
                pairs.append((source, plain.at[j, at(start, rows, 16), :]))
            continue
        for number in range(2):
            source = parts[2 + 2 * (s - 2) + number]
            first = blocks * ((idx[0] ^ number) & 1)
            for q in range(blocks):
                place = first + q
                target = plain.at[
                    lax.div(place, 2), at(start + lax.rem(place, 2) * part, part, 16), :
                ]
                pairs.append((source.at[q * part : (q + 1) * part, :], target))
    fetch(pairs, sems)
    width = plain.shape[1]
    for j in range(blocks):
        for k in range(5):
            turned = jnp.transpose(plain[j, :, k * width : (k + 1) * width])
            if k < 3:
                dil_t[j, :, k * width : (k + 1) * width] = turned
            else:
                point_t[j, :, (k - 3) * width : (k - 2) * width] = turned


def up_kernel(pieces, idx, *refs):
    mains, sides = refs[:pieces], refs[pieces : 2 * pieces]
    up_v, up_sq, up_g, up_b, frame_id, order = refs[2 * pieces : 2 * pieces + 6]
    outs = refs[2 * pieces + 6 : 3 * pieces + 6]
    act_hbm, up_hbm = refs[3 * pieces + 6 : 3 * pieces + 8]
    raw, stacked, phases, wide, act_out, up_w, sems, out_sems = refs[3 * pieces + 8 :]
    rows, frames = mains[0].shape
    local_out = up_v.shape[1]
    copies = []
    for s in range(pieces):
        here = at((idx[1] ^ s) * rows, rows, 16)
        for source, target in (
            (sides[s].at[:, 0:LANES], raw.at[here, 0:LANES]),
            (mains[s], raw.at[here, LANES : LANES + frames]),
            (sides[s].at[:, LANES:], raw.at[here, LANES + frames :]),
        ):
            copies.append(pltpu.make_async_copy(source, target, sems.at[len(copies)]))
            copies[-1].start()
    norm = jnp.sqrt(up_sq[...])
    for k in range(up_v.shape[0]):
        up_w[k * local_out : (k + 1) * local_out, :] = (up_g[...] * up_v[k] / norm).astype(BF)
    kept = [
        pltpu.make_async_copy(up_w, up_hbm, out_sems.at[pieces]),
        pltpu.make_async_copy(act_out, act_hbm, out_sems.at[pieces + 1]),
    ]
    kept[0].start()
    for copy in copies:
        copy.wait()
    total = frames + 2 * LANES
    count = stacked.shape[1]
    channels = raw.shape[0]
    shift = total - (LANES - HALO // 8)
    ids = pltpu.roll(jnp.broadcast_to(frame_id[...], (8, total)), shift, axis=1)
    before = pltpu.roll(ids, 1, axis=1)
    after = pltpu.roll(ids, total - 1, axis=1)
    left = jnp.where(before == ids, 1.0, 0.0)[0:1, :].astype(BF)
    right = jnp.where(after == ids, 1.0, 0.0)[0:1, :].astype(BF)
    step = channels
    for r0 in range(0, channels, step):
        part = pl.ds(r0, step)
        acted = unit_act(raw[part, :].astype(F32)).astype(BF)
        act_out[part, :] = acted[:, LANES : LANES + frames]
        moved = pltpu.roll(acted, shift, axis=1)
        one = pltpu.roll(moved, 1, axis=1) * left
        two = pltpu.roll(moved, total - 1, axis=1) * right
        stacked[part, :] = moved[:, 0:count]
        stacked[pl.ds(channels + r0, step), :] = one[:, 0:count]
        stacked[pl.ds(2 * channels + r0, step), :] = two[:, 0:count]
    kept[1].start()
    eye = eye_mask(local_out)
    bias = to_col(up_b[...], eye)
    bias4 = jnp.concatenate([bias] * 4, axis=0)
    quarter = 4 * local_out
    for c0 in range(0, count, 3 * LANES):
        cols = pl.ds(c0, 3 * LANES)
        center = stacked[0:channels, cols]
        low = dot(up_w[quarter : 2 * quarter, :], center)
        low = low + dot(up_w[3 * quarter : 4 * quarter, :], stacked[channels : 2 * channels, cols])
        high = dot(up_w[2 * quarter : 3 * quarter, :], center)
        high = high + dot(up_w[0:quarter, :], stacked[2 * channels : 3 * channels, cols])
        low = (low + bias4).astype(BF)
        high = (high + bias4).astype(BF)
        for b in range(3):
            block = c0 // LANES + b
            if block * local_out >= phases.shape[0]:
                continue
            for r in range(8):
                source = (low, high)[r // 4]
                phases[block * local_out : (block + 1) * local_out, r * LANES : (r + 1) * LANES] = (
                    source[
                        (r % 4) * local_out : (r % 4 + 1) * local_out,
                        b * LANES : (b + 1) * LANES,
                    ]
                )
    turned = dot(phases[...], order[...]).astype(BF)
    for block in range(count // LANES):
        wide[:, block * 1024 : (block + 1) * 1024] = turned[
            block * local_out : (block + 1) * local_out, :
        ]
    own = 8 * frames // pieces
    fetch(
        [
            (wide.at[:, at((idx[1] ^ s) * own, own + 2 * HALO, LANES)], outs[s])
            for s in range(pieces)
        ],
        out_sems,
    )
    for copy in kept:
        copy.wait()


def sample_masks(sample_id, distance):
    width = sample_id.shape[1]
    ids = jnp.broadcast_to(sample_id[...], (8, width))
    back = pltpu.roll(ids, distance, axis=1)
    ahead = pltpu.roll(ids, width - distance, axis=1)
    return (
        jnp.where(back == ids, 1.0, 0.0)[0:1, :].astype(BF),
        jnp.where(ahead == ids, 1.0, 0.0)[0:1, :].astype(BF),
    )


def forward_kernel(pieces, blocks, idx, *refs):
    parts = refs[:pieces]
    plain, sample_id, silence = refs[pieces : pieces + 3]
    outs = refs[pieces + 3 : 2 * pieces + 3]
    kept = refs[2 * pieces + 3 : 2 * pieces + 8]
    hidden, taps, pair, final, sems, out_sems = refs[2 * pieces + 8 :]
    keep_h, keep_u, keep_m, keep_sh, keep_sc = kept
    rows, width = parts[0].shape
    channels = pieces * rows
    fetch(
        [(parts[s], hidden.at[at((idx[1] ^ s) * rows, rows, 16), :]) for s in range(pieces)], sems
    )
    for j in range(blocks):
        distance = 3**j
        tail = plain[j, :, 5 * channels : 5 * channels + TAIL].astype(F32)
        dil_b = tail[:, 0:1] + tail[:, 1:2]
        out_b = tail[:, 2:3] + tail[:, 3:4]

        low = hidden[...]
        keep_h[j] = low
        pair[channels : 2 * channels, :] = low
        acted, slope = unit(low.astype(F32))
        acted = acted.astype(BF)
        taps[channels : 2 * channels, :] = acted
        keep_u[j] = acted
        keep_sh[j] = slope.astype(BF)
        back, ahead = sample_masks(sample_id, distance)
        center = taps[channels : 2 * channels, :]
        taps[0:channels, :] = pltpu.roll(center, distance, axis=1) * back
        taps[2 * channels : 3 * channels, :] = pltpu.roll(center, width - distance, axis=1) * ahead

        inner = dot(plain[j, :, 0 : 3 * channels], taps[...]) + dil_b
        acted, slope = unit(inner)
        acted = acted.astype(BF)
        pair[0:channels, :] = acted
        keep_m[j] = acted
        keep_sc[j] = slope.astype(BF)
        after = dot(plain[j, :, 3 * channels : 5 * channels], pair[...]) + out_b
        if j < blocks - 1:
            hidden[...] = after.astype(BF)
        else:
            final[...] = after
    own = width - 2 * HALO
    voiced = silence[:, at(idx[1] * own, own, LANES)].astype(F32)
    hidden[:, 0:own] = (final[:, HALO : HALO + own] * voiced).astype(BF)
    fetch(
        [
            (hidden.at[at((idx[1] ^ s) * rows, rows, 16), 0:own], outs[s])
            for s in range(pieces)
        ],
        out_sems,
    )


def spread_taps(j, center, sample_id, taps):
    channels, width = center.shape
    distance = 3**j
    back, ahead = sample_masks(sample_id, distance)
    taps[channels : 2 * channels, :] = center
    taps[0:channels, :] = pltpu.roll(center, width - distance, axis=1) * ahead
    taps[2 * channels : 3 * channels, :] = pltpu.roll(center, distance, axis=1) * back


def edge_start(pieces, peer):
    return jnp.where(peer < pieces // 2, 0, HALO)


def backward_kernel(pieces, idx, *refs):
    parts = refs[:pieces]
    dil_t, point_t, sample_id, keep_sh, keep_sc = refs[pieces : pieces + 5]
    outs = refs[pieces + 5 : 2 * pieces + 5]
    errs, inners, taps, low, sems, out_sems = refs[2 * pieces + 5 :]
    rows = parts[0].shape[0]
    blocks, channels, width = errs.shape
    last = blocks - 1
    fetch(
        [(parts[s], errs.at[last, at((idx[1] ^ s) * rows, rows, 16), :]) for s in range(pieces)],
        sems,
    )
    for j in reversed(range(blocks)):
        err = errs[j]
        inner = dot(point_t[j, :, 0:channels], err) * keep_sc[j].astype(F32)
        inner = inner.astype(BF)
        inners[j] = inner
        spread_taps(j, inner, sample_id, taps)
        spread = dot(dil_t[j], taps[...]) * keep_sh[j].astype(F32)
        after = (spread + dot(point_t[j, :, channels : 2 * channels], err)).astype(BF)
        if j > 0:
            errs[j - 1] = after
        else:
            low[...] = after
    lanes = at(edge_start(pieces, idx[1]), width - HALO, LANES)
    fetch(
        [(low.at[at((idx[1] ^ s) * rows, rows, 16), lanes], outs[s]) for s in range(pieces)],
        out_sems,
    )


def grad_kernel(pieces, order, idx, errs, inners, sample_id, keep_h, keep_u, keep_m, *refs):
    keep, send, taps, mats, sems = refs
    blocks, channels, width = errs.shape
    inside = pl.ds(HALO, width - 2 * HALO)
    rows = channels // pieces
    lane = lax.broadcasted_iota(jnp.int32, (channels, channels), 1)
    tail = jnp.zeros((channels, channels), F32)
    size = mats.shape[0] * rows
    copies = []

    def ship(m):
        for position, s in enumerate(order):
            target = (keep, send)[position // (pieces // 2)]
            start = position % (pieces // 2) * size + m * rows
            copies.append(
                pltpu.make_async_copy(
                    mats.at[m, at((idx[1] ^ s) * rows, rows, 16), :],
                    target.at[start : start + rows, :],
                    sems.at[len(copies)],
                )
            )
            copies[-1].start()

    for j in range(blocks):
        spread_taps(j, inners[j], sample_id, taps)
        err = errs[j, :, inside]
        mats[5 * j + 3] = dot_rt(err, keep_m[j, :, inside]).astype(BF)
        ship(5 * j + 3)
        mats[5 * j + 4] = dot_rt(err, keep_h[j, :, inside]).astype(BF)
        ship(5 * j + 4)
        for k in range(3):
            mats[5 * j + k] = dot_rt(
                taps[k * channels : (k + 1) * channels, inside], keep_u[j, :, inside]
            ).astype(BF)
            ship(5 * j + k)
        dil_sum = jnp.sum(inners[j, :, inside].astype(F32), axis=1, keepdims=True)
        out_sum = jnp.sum(err.astype(F32), axis=1, keepdims=True)
        tail = tail + jnp.where(lane == 2 * j, dil_sum, 0.0)
        tail = tail + jnp.where(lane == 2 * j + 1, out_sum, 0.0)
    mats[5 * blocks] = tail.astype(BF)
    ship(5 * blocks)
    for copy in copies:
        copy.wait()


def halve_kernel(idx, keep, got, next_keep, next_send):
    half = next_keep.shape[0]
    total = keep[...].astype(F32) + got[...].astype(F32)
    next_keep[...] = total[:half].astype(BF)
    next_send[...] = total[half:].astype(BF)


def up_back_kernel(pieces, peers, orders, idx, *refs):
    parts = refs[:pieces]
    up_v, acted, frame_id, order = refs[pieces : pieces + 4]
    cols_grad, *streams = refs[pieces + 4 : pieces + 9]
    wide, stacked, phases, low_grad, sems = refs[pieces + 9 :]
    rows = parts[0].shape[0]
    own = parts[0].shape[1] - HALO
    length = pieces * own
    frames = length // 8
    copies = []
    for s in range(pieces):
        peer = idx[1] ^ s
        target = wide.at[:, at(HALO + peer * own, own, LANES)]
        source = parts[s].at[:, at(HALO - edge_start(pieces, peer), own, LANES)]
        copies.append(pltpu.make_async_copy(source, target, sems.at[s]))
        copies[-1].start()
    wide[:, HALO + length :] = jnp.zeros((rows, wide.shape[1] - HALO - length), BF)
    for copy in copies:
        copy.wait()
    for s in range(pieces):
        peer = idx[1] ^ s

        @pl.when(peer == 0)
        def _():
            pltpu.sync_copy(parts[s].at[:, 0:HALO], wide.at[:, 0:HALO])

        @pl.when(peer == pieces - 1)
        def _():
            pltpu.sync_copy(
                parts[s].at[:, own:], wide.at[:, HALO + length : 2 * HALO + length]
            )

    total = wide.shape[1] // 8
    blocks = total // LANES
    for block in range(blocks):
        stacked[block * rows : (block + 1) * rows, :] = wide[:, block * 1024 : (block + 1) * 1024]
    turned = dot_rt(stacked[...], order[...]).astype(BF)
    for block in range(blocks):
        for r in range(8):
            phases[r * rows : (r + 1) * rows, block * LANES : (block + 1) * LANES] = turned[
                block * rows : (block + 1) * rows, r * LANES : (r + 1) * LANES
            ]
    ids = jnp.broadcast_to(frame_id[...], (8, frame_id.shape[1]))
    before = pltpu.roll(ids, 1, axis=1)
    after = pltpu.roll(ids, frame_id.shape[1] - 1, axis=1)
    inside = slice(LANES, LANES + frames)
    left = jnp.where(before == ids, 1.0, 0.0)[0:1, inside]
    right = jnp.where(after == ids, 1.0, 0.0)[0:1, inside]
    lead = HALO // 8
    eighth = 4 * rows
    sample_sum = jnp.zeros((rows, 1), F32)
    for part in range(2):
        base = phases[part * eighth : (part + 1) * eighth, :]
        center = pltpu.roll(base, total - lead, axis=1)[:, 0:frames]
        cols_grad[(4 + 4 * part) * rows : (8 + 4 * part) * rows, :] = center
        partial = jnp.sum(center.astype(F32), axis=1, keepdims=True)
        for r in range(4):
            sample_sum = sample_sum + partial[r * rows : (r + 1) * rows]
        if part == 1:
            moved = pltpu.roll(base, total - lead + 1, axis=1)[:, 0:frames]
            cols_grad[0:eighth, :] = (moved.astype(F32) * left).astype(BF)
        else:
            moved = pltpu.roll(base, total - lead - 1, axis=1)[:, 0:frames]
            cols_grad[12 * rows : 16 * rows, :] = (moved.astype(F32) * right).astype(BF)
    taps = up_v.shape[0]
    channels = up_v.shape[2]
    inner = jnp.zeros((rows, channels), F32)
    grad = dot_rt(cols_grad[...], acted[...])
    low_grad[...] = grad.astype(BF)
    for k in range(taps):
        inner = inner + grad[k * rows : (k + 1) * rows] * up_v[k]
    inner = jnp.sum(inner, axis=0, keepdims=True)
    bias = jnp.concatenate(
        [to_row(sample_sum, eye_mask(rows)), jnp.zeros((1, channels - rows), F32)], axis=1
    )
    side = channels // 2
    line = lax.broadcasted_iota(jnp.int32, (SUMS, side), 0)
    sums = jnp.zeros((SUMS, side), F32)
    for number, value in enumerate((inner[:, :side], inner[:, side:], bias[:, :side])):
        high = value.astype(BF).astype(F32)
        sums = sums + jnp.where(line == 2 * number, high, 0.0)
        sums = sums + jnp.where(line == 2 * number + 1, value - high, 0.0)
    half = peers // 2
    size = streams[2].shape[0] // half
    streams[0][half * size :, :] = sums.astype(BF)
    streams[1][half * size :, :] = sums.astype(BF)
    for number, sequence in enumerate(orders):
        lanes = pl.ds(number * side, side)
        for position, s in enumerate(sequence):
            target = streams[2 * number + position // half]
            start = position % half * size
            target[start : start + size, :] = low_grad[at((idx[0] ^ s) * size, size, 16), lanes]


def input_back_kernel(pieces, order, idx, up_w, cols_grad, keep, send, total, sems):
    total[...] = lax.dot_general(
        up_w[...], cols_grad[...], (((0,), (0,)), ((), ())), preferred_element_type=F32
    ).astype(BF)
    size = total.shape[0] // pieces
    pairs = []
    for position, s in enumerate(order):
        target = (keep, send)[position // (pieces // 2)]
        start = position % (pieces // 2) * size
        pairs.append(
            (total.at[at((idx[1] ^ s) * size, size, 16), :], target.at[start : start + size, :])
        )
    fetch(pairs, sems)


def join_kernel(order, idx, keep, got, term, other, next_keep, next_send, whole):
    rows = keep.shape[0] - SUMS
    half = rows // 2
    total = keep[...].astype(F32) + got[...].astype(F32)
    whole[...] = (term[...].astype(F32) + other[...].astype(F32)).astype(BF)
    sums = total[rows:].astype(BF)
    size = whole.shape[0] // len(order)
    count = len(order) // 2
    for number, target in enumerate((next_keep, next_send)):
        target[0:half, :] = total[number * half : (number + 1) * half].astype(BF)
        for position in range(count):
            s = order[number * count + position]
            start = half + position * size
            target[start : start + size, :] = whole[
                at(((idx[0] ^ s) >> 1) * size, size, 16), :
            ]
        target[half + count * size :, :] = sums


def step_kernel(rows, last, idx, keep, got, *outs):
    total = keep[...].astype(F32) + got[...].astype(F32)
    grads = total.shape[0] - rows - SUMS
    if last:
        outs[0][...] = total[:rows].astype(BF)
        outs[1][...] = total[rows : rows + grads].astype(BF)
        outs[2][...] = total[rows + grads :]
        return
    for number, target in enumerate(outs):
        half, part = rows // 2, grads // 2
        target[0:half, :] = total[number * half : (number + 1) * half].astype(BF)
        start = rows + number * part
        target[half : half + part, :] = total[start : start + part].astype(BF)
        target[half + part :, :] = total[rows + grads :].astype(BF)


def meet_kernel(idx, keep, got, grads, out):
    rows = keep.shape[0]
    out[0:rows, :] = (keep[...].astype(F32) + got[...].astype(F32)).astype(BF)
    out[rows:, :] = grads[...]


def double_kernel(rows, add, idx, own, got, out):
    grads = own.shape[0] - rows
    out[0:rows, :] = own[0:rows, :]
    out[rows : 2 * rows, :] = got[0:rows, :]
    if add:
        out[2 * rows :, :] = (own[rows:, :].astype(F32) + got[rows:, :].astype(F32)).astype(BF)
    else:
        out[2 * rows : 2 * rows + grads, :] = own[rows:, :]
        out[2 * rows + grads :, :] = got[rows:, :]


def final_kernel(orders, grad_order, offset, idx, *refs):
    streams = refs[:4]
    up_v, up_sq, up_g, inner_sum, dil_v, dil_g, mix_v, mix_g, skip_v, skip_g = refs[4:14]
    up_v_grad, up_g_grad, *outs = refs[14:24]
    whole, blocks_whole, staged, *block_staged, in_sems, grad_sems, out_sems = refs[24:]
    half = len(orders[0]) // 2
    size = whole.shape[0] // (2 * half)
    side = whole.shape[1] // 2
    copies = []
    for number, sequence in enumerate(orders):
        for position, s in enumerate(sequence):
            source = streams[2 * number + position // half]
            start = position % half * size
            target = whole.at[
                at((idx[0] ^ s) * size, size, 16), number * side : (number + 1) * side
            ]
            copies.append(
                pltpu.make_async_copy(
                    source.at[start : start + size, :], target, in_sems.at[len(copies)]
                )
            )
            copies[-1].start()
    grad_half = len(grad_order) // 2
    size = blocks_whole.shape[0] // len(grad_order)
    grads = []
    for position, s in enumerate(grad_order):
        start = offset + position % grad_half * size
        grads.append(
            pltpu.make_async_copy(
                streams[2 + position // grad_half].at[start : start + size, :],
                blocks_whole.at[at(((idx[0] ^ s) >> 1) * size, size, 16), :],
                grad_sems.at[len(grads)],
            )
        )
        grads[-1].start()
    for copy in copies:
        copy.wait()
    sent = []

    def ship(source, target):
        sent.append(pltpu.make_async_copy(source, target, out_sems.at[len(sent)]))
        sent[-1].start()

    norm = jnp.sqrt(up_sq[...])
    inner = inner_sum[...]
    scale = up_g[...] / norm
    pull = up_g[...] * inner / (norm * norm * norm)
    rows = up_v.shape[1]
    for k in range(up_v.shape[0]):
        grad = whole[k * rows : (k + 1) * rows, :].astype(F32)
        staged[k] = scale * grad - pull * up_v[k]
        ship(staged.at[k], up_v_grad.at[k])
    up_g_grad[...] = inner / norm
    for copy in grads:
        copy.wait()
    dil_v_hbm, dil_g_out, dil_b_out, mix_v_hbm, mix_g_out, out_b_out, skip_v_hbm, skip_g_out = outs
    dil_v_out, mix_v_out, skip_v_out = block_staged
    eye = eye_mask(rows)
    blocks = dil_v.shape[0]
    tail = blocks_whole[5 * blocks * rows :, :].astype(F32)
    for j in range(blocks):

        def mat(m):
            start = (5 * j + m) * rows
            return blocks_whole[start : start + rows, :].astype(F32)

        square = jnp.zeros((rows, 1), F32)
        inner = jnp.zeros((rows, 1), F32)
        for k in range(3):
            v = dil_v[j, k]
            square = square + jnp.sum(v * v, axis=1, keepdims=True)
            inner = inner + jnp.sum(v * mat(k), axis=1, keepdims=True)
        norm = jnp.sqrt(square)
        gain = to_col(dil_g[j : j + 1, :], eye)
        for k in range(3):
            dil_v_out[j, k] = gain / norm * mat(k) - gain * inner / (norm**3) * dil_v[j, k]
        ship(dil_v_out.at[j], dil_v_hbm.at[j])
        dil_g_out[j : j + 1, :] = to_row(inner / norm, eye)
        for number, (vref, gref, v_out, v_hbm, g_out) in enumerate(
            (
                (mix_v, mix_g, mix_v_out, mix_v_hbm, mix_g_out),
                (skip_v, skip_g, skip_v_out, skip_v_hbm, skip_g_out),
            )
        ):
            v = vref[j]
            grad = mat(3 + number)
            norm = jnp.sqrt(jnp.sum(v * v, axis=1, keepdims=True))
            inner = jnp.sum(v * grad, axis=1, keepdims=True)
            gain = to_col(gref[j : j + 1, :], eye)
            v_out[j] = gain / norm * grad - gain * inner / (norm**3) * v
            ship(v_out.at[j], v_hbm.at[j])
            g_out[j : j + 1, :] = to_row(inner / norm, eye)
        dil_b_out[j : j + 1, :] = to_row(tail[:, 2 * j : 2 * j + 1], eye)
        out_b_out[j : j + 1, :] = to_row(tail[:, 2 * j + 1 : 2 * j + 2], eye)
    for copy in sent:
        copy.wait()


def place_kernel(pieces, idx, *refs):
    parts, out, sems = refs[:pieces], refs[pieces], refs[pieces + 1]
    own = parts[0].shape[1]
    fetch(
        [(parts[s], out.at[:, at((idx[1] ^ s) * own, own, LANES)]) for s in range(pieces)], sems
    )


def input_kernel(idx, *refs):
    *terms, spectrogram, out = refs
    total = terms[0][...].astype(F32)
    for term in terms[1:]:
        total = total + term[...].astype(F32)
    out[...] = (total * unit(spectrogram[...].astype(F32))[1]).astype(BF)


def local(
    spectrogram_input,
    upsample_direction,
    upsample_magnitude,
    upsample_bias,
    dilated_direction,
    dilated_magnitude,
    dilated_bias,
    pointwise_direction,
    pointwise_magnitude,
    block_output_bias,
    shortcut_direction,
    shortcut_magnitude,
    cotangent,
    silence,
    segments,
):
    pieces, peers = lax.axis_size("chan"), lax.axis_size("tm")
    chan, tm = lax.axis_index("chan"), lax.axis_index("tm")
    in_rows, frames = spectrogram_input.shape
    taps, rows, in_channels = upsample_direction.shape
    blocks = dilated_direction.shape[0]
    channels = dilated_direction.shape[3]
    length = 8 * frames
    own = length // pieces
    width = own + 2 * HALO
    packed_width = 5 * channels + TAIL
    forward = [(k, k + 1) for k in range(peers - 1)]
    backward = [(k + 1, k) for k in range(peers - 1)]
    dma = pltpu.SemaphoreType.DMA
    lead = HALO // 8
    tie = lax.optimization_barrier

    silence_row = silence.reshape(1, length)
    up_g = upsample_magnitude.reshape(1, in_channels)
    edge_rows = in_rows + rows
    ahead, behind = kernel_call(
        edge_kernel,
        [((edge_rows, LANES), BF, "V")] * 2,
        [spectrogram_input, cotangent, silence_row],
        "HHH",
        scratch=[
            pltpu.VMEM((in_rows, LANES), BF),
            pltpu.VMEM((in_rows, LANES), BF),
            pltpu.VMEM((2, rows, HALO), BF),
            pltpu.VMEM((2, 1, HALO), jnp.int32),
            dma((6,)),
        ],
    )
    low_edge = lax.ppermute(ahead, "tm", forward)
    high_edge = lax.ppermute(behind, "tm", backward)
    all_mains = gather_chan(spectrogram_input)
    up_v_late, ahead = tie((upsample_direction, ahead))
    (up_sq,) = kernel_call(
        square_kernel, [((1, in_channels), F32, "V")], [up_v_late], "F", micros=2
    )
    block_args = [
        dilated_direction,
        dilated_magnitude,
        dilated_bias,
        pointwise_direction,
        pointwise_magnitude,
        block_output_bias,
        shortcut_direction,
        shortcut_magnitude,
    ]
    sides = jnp.concatenate([low_edge[:in_rows], high_edge[:in_rows]], axis=1)
    block_args, sides = tie((block_args, sides))
    packed_half = ((blocks * rows // 2, packed_width), BF, "V")
    packed, near, far, order = kernel_call(
        prep_kernel,
        [((blocks * rows, packed_width), BF, "V"), packed_half, packed_half]
        + [((8 * LANES, 8 * LANES), BF, "H")],
        block_args,
        "FFFFFFFF",
        scratch=[pltpu.VMEM((8 * LANES, 8 * LANES), BF), dma],
        micros=3,
    )
    all_sides = gather_chan(sides)
    for bit in bits_of(pieces):
        up_sq = up_sq + swap(up_sq, "chan", bit)
    padded_ids = jnp.pad(segments.astype(F32), LANES, constant_values=-1.0)
    frame_id = lax.dynamic_slice_in_dim(padded_ids, tm * frames, frames + 2 * LANES)
    sample_id = jnp.repeat(
        lax.dynamic_slice_in_dim(
            padded_ids, LANES + tm * frames + chan * (own // 8) - lead, width // 8
        ),
        8,
    ).reshape(1, width)
    frame_id = frame_id.reshape(1, frames + 2 * LANES)
    near, low_edge = tie((near, low_edge))
    cut = kernel_call(
        functools.partial(cut_kernel, pieces),
        [((rows, width), BF, "H")] * pieces,
        [cotangent, silence_row, low_edge, high_edge],
        "FFGG",
        scratch=[pltpu.VMEM((rows, length + 2 * HALO), BF), dma((pieces,))],
        micros=2,
    )
    top = pieces // 2
    near, cut, all_sides[top], up_sq = tie((near, list(cut), all_sides[top], up_sq))

    count = -(-(frames + 2 * lead) // LANES) * LANES
    count = -(-count // (3 * LANES)) * 3 * LANES
    up_outs = kernel_call(
        functools.partial(up_kernel, pieces),
        [((rows, width), BF, "H")] * pieces
        + [((in_channels, frames), BF, "H"), ((taps * rows, in_channels), BF, "H")],
        all_mains
        + all_sides
        + [upsample_direction, up_sq, up_g, upsample_bias.reshape(1, rows), frame_id, order],
        "A" * (2 * pieces) + "FGFFGF",
        scratch=[
            pltpu.VMEM((in_channels, frames + 2 * LANES), BF),
            pltpu.VMEM((3 * in_channels, count), BF),
            pltpu.VMEM((count // LANES * rows, 8 * LANES), BF),
            pltpu.VMEM((rows, 8 * count), BF),
            pltpu.VMEM((in_channels, frames), BF),
            pltpu.VMEM((taps * rows, in_channels), BF),
            dma((3 * pieces,)),
            dma((pieces + 2,)),
        ],
        micros=6,
    )
    acted, up_w = up_outs[pieces:]
    chan_bits = bits_of(pieces)
    held_near = {0: near}
    for bit in reversed(chan_bits[1:]):
        for slot in list(held_near):
            held_near[slot ^ bit] = swap(held_near[slot], "chan", bit)
    all_packed = [packed, swap(packed, "chan", 1)]
    for slot in range(2, pieces, 2):
        two = [held_near[slot], swap(held_near[slot], "tm", 1)]
        all_packed += two + [swap(value, "chan", 1) for value in two]
    all_hidden = exchange_chan(list(up_outs[:pieces]))
    all_packed, all_hidden[top] = tie((all_packed, all_hidden[top]))

    plain, dil_t, point_t = kernel_call(
        functools.partial(weight_kernel, pieces, blocks),
        [
            ((blocks, channels, packed_width), BF, "R"),
            ((blocks, channels, 3 * channels), BF, "R"),
            ((blocks, channels, 2 * channels), BF, "R"),
        ],
        all_packed,
        "A" * len(all_packed),
        scratch=[dma((2 * blocks * pieces,))],
        micros=3,
    )
    cut, all_hidden = tie((cut, all_hidden))
    all_err = exchange_chan(cut)

    kept_shape = ((blocks, channels, width), BF, "R")
    forward_outs = kernel_call(
        functools.partial(forward_kernel, pieces, blocks),
        [((rows, own), BF, "H")] * pieces + [kept_shape] * 5,
        all_hidden + [plain, sample_id, silence_row],
        "A" * pieces + "RGF",
        scratch=[
            pltpu.VMEM((channels, width), BF),
            pltpu.VMEM((3 * channels, width), BF),
            pltpu.VMEM((2 * channels, width), BF),
            pltpu.VMEM((channels, width), F32),
            dma((pieces,)),
            dma((pieces,)),
        ],
        micros=10,
    )
    keep_h, keep_u, keep_m, keep_sh, keep_sc = forward_outs[pieces:]
    activation_parts = list(forward_outs[:pieces])

    backward_outs = kernel_call(
        functools.partial(backward_kernel, pieces),
        [((rows, width - HALO), BF, "H")] * pieces + [kept_shape] * 2,
        all_err + [dil_t, point_t, sample_id, keep_sh, keep_sc],
        "A" * pieces + "RRGRR",
        scratch=[
            pltpu.VMEM((3 * channels, width), BF),
            pltpu.VMEM((channels, width), BF),
            dma((pieces,)),
            dma((pieces,)),
        ],
        micros=10,
    )
    errs, inners = backward_outs[pieces:]
    all_low = exchange_chan(list(backward_outs[:pieces]))
    errs, all_low[top] = tie((errs, all_low[top]))

    chan_order = order_of(chan_bits)
    mats = 5 * blocks + 1
    share = pieces // 2 * mats * rows
    keep, send = kernel_call(
        functools.partial(grad_kernel, pieces, chan_order),
        [((share, channels), BF, "H")] * 2,
        [errs, inners, sample_id, keep_h, keep_u, keep_m],
        "RRGRRR",
        scratch=[
            pltpu.VMEM((3 * channels, width), BF),
            pltpu.VMEM((mats, channels, channels), BF),
            dma((mats * pieces,)),
        ],
        micros=8,
    )

    def scatter_chan(keep, send):
        for bit in chan_bits[:-1]:
            got = swap(send, "chan", bit)
            next_shape = ((keep.shape[0] // 2, keep.shape[1]), BF, "V")
            keep, send = kernel_call(halve_kernel, [next_shape] * 2, [keep, got], "GG")
        return keep, swap(send, "chan", chan_bits[-1])

    block_terms = scatter_chan(keep, send)

    tm_bits = bits_of(peers)
    turned_bits = tm_bits[1:] + tm_bits[:1]
    orders = (order_of(tm_bits), order_of(turned_bits))
    half = peers // 2
    total_rows = taps * rows
    size = total_rows // peers
    side = in_channels // 2
    cols_grad, keep_one, send_one, keep_two, send_two = kernel_call(
        functools.partial(up_back_kernel, pieces, peers, orders),
        [((total_rows, frames), BF, "R")]
        + [((half * size + SUMS, side), BF, "V")] * 2
        + [((half * size, side), BF, "V")] * 2,
        all_low + [upsample_direction, acted, frame_id, order],
        "A" * pieces + "FFGF",
        scratch=[
            pltpu.VMEM((rows, 8 * count), BF),
            pltpu.VMEM((count // LANES * rows, 8 * LANES), BF),
            pltpu.VMEM((8 * rows, count), BF),
            pltpu.VMEM((total_rows, in_channels), BF),
            dma((pieces,)),
        ],
        micros=5,
    )

    steps = len(tm_bits)
    grad_order = order_of(tm_bits[1:])
    block_rows = mats * rows
    one_rows, two_rows = half * size, half * size
    grads = None
    for step in range(steps):
        got_one = swap(send_one, "tm", tm_bits[step])
        got_two = swap(send_two, "tm", turned_bits[step])
        got_one, got_two = tie((got_one, got_two))
        last = step == steps - 1
        if step == 0:
            next_rows = one_rows // 2 + block_rows // 2 + SUMS
            keep_one, send_one = kernel_call(
                functools.partial(join_kernel, grad_order),
                [((next_rows, side), BF, "V")] * 2,
                [keep_one, got_one, *block_terms],
                "GGGG",
                scratch=[pltpu.VMEM((block_rows, side), BF)],
            )
            one_rows, block_rows = one_rows // 2, block_rows // 2
        elif not last:
            next_rows = one_rows // 2 + block_rows // 2 + SUMS
            keep_one, send_one = kernel_call(
                functools.partial(step_kernel, one_rows, False),
                [((next_rows, side), BF, "V")] * 2,
                [keep_one, got_one],
                "GG",
            )
            one_rows, block_rows = one_rows // 2, block_rows // 2
        else:
            own_one, grads, sums = kernel_call(
                functools.partial(step_kernel, one_rows, True),
                [((one_rows, side), BF, "V"), ((block_rows, side), BF, "V")]
                + [((SUMS, side), F32, "V")],
                [keep_one, got_one],
                "GG",
            )
        if not last:
            two_rows = two_rows // 2
            keep_two, send_two = kernel_call(
                halve_kernel, [((two_rows, side), BF, "V")] * 2, [keep_two, got_two], "GG"
            )
        else:
            (own_two,) = kernel_call(
                meet_kernel,
                [((two_rows + block_rows, side), BF, "V")],
                [keep_two, got_two, grads],
                "GGG",
            )
    for step in reversed(range(steps)):
        got_one = swap(own_one, "tm", tm_bits[step])
        got_two = swap(own_two, "tm", turned_bits[step])
        got_one, got_two = tie((got_one, got_two))
        if step > 0:
            own_one = jnp.concatenate([own_one, got_one], axis=0)
            add = step == steps - 1
            grown = 2 * two_rows + (block_rows if add else 2 * block_rows)
            (own_two,) = kernel_call(
                functools.partial(double_kernel, two_rows, add),
                [((grown, side), BF, "V")],
                [own_two, got_two],
                "GG",
            )
            two_rows = 2 * two_rows
            block_rows = block_rows if add else 2 * block_rows

    pair = sums[0:6:2] + sums[1:6:2]
    inner_sum = pair[0:2].reshape(1, in_channels)
    for bit in chan_bits:
        inner_sum = inner_sum + swap(inner_sum, "chan", bit)

    piece_rows = pieces // 2 * in_rows
    keep, send = kernel_call(
        functools.partial(input_back_kernel, pieces, chan_order),
        [((piece_rows, frames), BF, "H")] * 2,
        [up_w, cols_grad],
        "FR",
        scratch=[pltpu.VMEM((in_channels, frames), BF), dma((pieces,))],
        micros=3,
    )
    input_terms = scatter_chan(keep, send)
    (input_grad,) = kernel_call(
        input_kernel,
        [((in_rows, frames), BF, "V")],
        [*input_terms, spectrogram_input],
        "GGF",
    )
    activation_parts, input_terms = tie((activation_parts, input_terms))
    activation_parts = exchange_chan(activation_parts)
    (activation,) = kernel_call(
        functools.partial(place_kernel, pieces),
        [((rows, length), BF, "V")],
        activation_parts,
        "A" * pieces,
        scratch=[dma((pieces,))],
        micros=2,
    )

    final_outs = kernel_call(
        functools.partial(final_kernel, orders, grad_order, two_rows),
        [
            (upsample_direction.shape, F32, "H"),
            ((1, in_channels), F32, "V"),
            (dilated_direction.shape, F32, "H"),
            (dilated_magnitude.shape, F32, "V"),
            (dilated_bias.shape, F32, "V"),
            (pointwise_direction.shape, F32, "H"),
            (pointwise_magnitude.shape, F32, "V"),
            (block_output_bias.shape, F32, "V"),
            (shortcut_direction.shape, F32, "H"),
            (shortcut_magnitude.shape, F32, "V"),
        ],
        [
            own_one,
            got_one,
            own_two,
            got_two,
            upsample_direction,
            up_sq,
            up_g,
            inner_sum,
            dilated_direction,
            dilated_magnitude,
            pointwise_direction,
            pointwise_magnitude,
            shortcut_direction,
            shortcut_magnitude,
        ],
        "AAAAFGFGFFFFFF",
        scratch=[
            pltpu.VMEM((total_rows, in_channels), BF),
            pltpu.VMEM((mats * rows, channels), BF),
            pltpu.VMEM(upsample_direction.shape, F32),
            pltpu.VMEM(dilated_direction.shape, F32),
            pltpu.VMEM(pointwise_direction.shape, F32),
            pltpu.VMEM(shortcut_direction.shape, F32),
            dma((2 * peers,)),
            dma((half,)),
            dma((taps + 3 * blocks,)),
        ],
        micros=5,
    )
    up_v_grad, up_g_grad, dil_v_grad, dil_g_grad, dil_b_grad = final_outs[:5]
    mix_v_grad, mix_g_grad, out_b_grad, skip_v_grad, skip_g_grad = final_outs[5:]
    return (
        activation,
        input_grad,
        up_v_grad,
        up_g_grad.reshape(in_channels),
        pair[2, :rows],
        dil_v_grad,
        dil_g_grad,
        dil_b_grad,
        mix_v_grad,
        mix_g_grad,
        out_b_grad,
        skip_v_grad,
        skip_g_grad,
    )


def solution(mesh):
    placed = (
        P("chan", "tm"),
        P(None, "chan", None),
        P(),
        P("chan"),
        P(None, None, "chan", None),
        P(None, "chan"),
        P(None, "chan"),
        P(None, "chan", None),
        P(None, "chan"),
        P(None, "chan"),
        P(None, "chan", None),
        P(None, "chan"),
        P("chan", "tm"),
        P("tm"),
        P(),
    )
    return jax.shard_map(
        local,
        mesh=mesh,
        in_specs=placed,
        out_specs=(
            P("chan", "tm"),
            P("chan", "tm"),
            P(None, "chan", None),
            P(),
            P("chan"),
            P(None, None, "chan", None),
            P(None, "chan"),
            P(None, "chan"),
            P(None, "chan", None),
            P(None, "chan"),
            P(None, "chan"),
            P(None, "chan", None),
            P(None, "chan"),
        ),
        check_vma=False,
    )
```

time: 320 us -> 187 us (0.58)
  blocking collectives: 67.2 us -> 0 us
  Pallas kernels: 103 us -> 67.2 us
  starting transfers between devices: 58.3 us -> 42.7 us
  local copies, waits for them, and re-layouts: 10.8 us -> 1.03 us
    psum x3 -> x0, blocking collectives: 67.2 us -> none  [the longest x1 38.4 us: local(): inner_sum = lax.psum(sums[:, :in_channels], ('tm', 'chan'))]
    pallas_call x11 -> x24, Pallas kernels: 103 us -> 67.2 us  [kernel_call(): pl.pallas_call(wrapped, out_shape=tuple(out_shape), in_specs=in_specs, ou...]
    ppermute x50 -> x43, starting transfers between devices: 48.9 us -> 35.8 us  [swap(): return lax.ppermute(values, axis, [(k, k ^ bit) for k in range(count)])]
    unnamed x99 -> x30, local copies, waits for them, and re-layouts: 7.28 us -> 0.08 us
    ppermute x4 -> x2, waiting for transfers between devices: 4.49 us -> 0.01 us  [the longest x1 0.01 us: local(): high_edge = lax.ppermute(behind, 'tm', backward)]
    ppermute x50 -> x43, waiting for transfers between devices: 70.7 us -> 73.5 us  [swap(): return lax.ppermute(values, axis, [(k, k ^ bit) for k in range(count)])]
    ppermute x4 -> x2, starting transfers between devices: 9.41 us -> 6.93 us  [the longest x1 5.63 us: local(): low_edge = lax.ppermute(ahead, 'tm', forward)]
  transfers between devices with their start and end apart: 54 -> 45, of which waited for: 16 -> 25; matrix products, arithmetic and copies ran while one was open for 2% -> 1% of each run, Pallas kernels for 30% -> 25%
where the time goes in v2:
time: 187 us; the launch traced here: 186 us
  waiting for transfers between devices  73.5 us (39%)
  Pallas kernels  67.2 us (36%)
  starting transfers between devices  42.7 us (23%)
    ppermute x43, waiting for transfers between devices, swap(): return lax.ppermute(values, axis, [(k, k ^ bit) for k in range(count)])  73.5 us
    pallas_call x24, Pallas kernels, kernel_call(): pl.pallas_call(wrapped, out_shape=tuple(out_shape), in_specs=in_specs, ou...  67.2 us
    ppermute x43, starting transfers between devices, swap(): return lax.ppermute(values, axis, [(k, k ^ bit) for k in range(count)])  35.8 us
    ppermute x1, starting transfers between devices, local(): low_edge = lax.ppermute(ahead, 'tm', forward)  5.63 us
  transfers between devices with their start and end apart: 45, of which 25 were waited for; matrix products, arithmetic and copies ran while one was open for 1% of the time, Pallas kernels for 25%

profile of v2, /device:TPU:0, one launch (start us, length us, event | category | flops | bytes accessed | tf_op | source)
XLA Modules:
  0.0 185.8 jit_solution(7581319533589767259)
XLA Ops:
  2.8 5.6 %collective-permute-start = (bf16[192,128]{1,0:T(8,128)(2,1)S(1)}, bf16[192,128]{1,0:T(8,128)(2,1)S(1)}, u32[]{:S(2)}, u32[]{:S(2)}) collective-permute-start(bf16[192,128]{1,0:T(8,128)(2,1)S(1)} %get-tuple-element.132), channel_id=1, source_target_pairs={{0,4},{4,8},{8,12},{12,16},{16,20},{20,24},{24,28},{1,5},{5,9},{9,... | collective-permute-start | bytes 147464 | tf_op jit(solution)/shard_map/ppermute | solution.py:849
  17.2 4.7 %shard_map.247 = (bf16[192,1408]{1,0:T(8,128)(2,1)S(1)}, bf16[96,1408]{1,0:T(8,128)(2,1)S(1)}, bf16[96,1408]{1,0:T(8,128)(2,1)}, bf16[1024,1024]{1,0:T(8,128)(2,1)}) custom-call(f32[3,3,64,256]{3,2,1,0:T(8,128)} %refs_8_.3, f32[3,64]{1,0:T(4,128)} %refs_9_.1, f32[3,64]{1,0:T(4,128)} %refs_2_.1, f32[3,64,256]{2,1,0:T(8,128)} %refs_10_.1, f32[3,64]{1,0:T(4,128)} %refs_11_.1, ...), custom_call_target="tpu_custom_call" | custom-call | flops 3300000000 | tf_op jit(solution)/shard_map/pallas_call | solution.py:91
  21.9 2.5 %shard_map.248 = (bf16[64,2304]{1,0:T(8,128)(2,1)}, bf16[64,2304]{1,0:T(8,128)(2,1)}, bf16[64,2304]{1,0:T(8,128)(2,1)}, bf16[64,2304]{1,0:T(8,128)(2,1)}) custom-call(bf16[64,8192]{1,0:T(8,128)(2,1)} %refs_0_.5, s32[1,8192]{1,0:T(1,128)} %bitcast.13, bf16[192,128]{1,0:T(8,128)(2,1)S(1)} %collective-permute-done.refs_2_, ...), custom_call_target="tpu_custom_call" | custom-call | flops 2200000000 | tf_op jit(solution)/shard_map/pallas_call | solution.py:91
  26.7 4.9 %collective-permute-done.12.refs_2_ = bf16[96,1408]{1,0:T(8,128)(2,1)S(1)} collective-permute-done((bf16[96,1408]{1,0:T(8,128)(2,1)S(1)}, bf16[96,1408]{1,0:T(8,128)(2,1)S(1)}, u32[]{:S(2)}, u32[]{:S(2)}) %collective-permute-start.12) | collective-permute-done | bytes 270368 | tf_op jit(solution)/shard_map/ppermute | solution.py:21
  34.0 7.5 %shard_map.250 = (bf16[64,2304]{1,0:T(8,128)(2,1)}, bf16[64,2304]{1,0:T(8,128)(2,1)}, bf16[64,2304]{1,0:T(8,128)(2,1)}, bf16[64,2304]{1,0:T(8,128)(2,1)}, bf16[5...) custom-call(bf16[128,1024]{1,0:T(8,128)(2,1)S(1)} %copy-done, bf16[128,1024]{1,0:T(8,128)(2,1)S(1)} %collective-permute-done.5.refs_1_, ...), custom_call_target="tpu_custom_call" | custom-call | flops 6600000000 | tf_op jit(solution)/shard_map/pallas_call | solution.py:91
  45.3 6.4 %collective-permute-done.16.refs_2_ = bf16[64,2304]{1,0:T(8,128)(2,1)S(1)} collective-permute-done((bf16[64,2304]{1,0:T(8,128)(2,1)}, bf16[64,2304]{1,0:T(8,128)(2,1)S(1)}, u32[]{:S(2)}, u32[]{:S(2)}) %collective-permute-start.16) | collective-permute-done | bytes 294944 | tf_op jit(solution)/shard_map/ppermute | solution.py:21
  56.0 3.8 %shard_map.251 = (bf16[3,256,1408]{2,1,0:T(8,128)(2,1)S(1)}, bf16[3,256,768]{2,1,0:T(8,128)(2,1)S(1)}, bf16[3,256,512]{2,1,0:T(8,128)(2,1)S(1)}) custom-call(bf16[192,1408]{1,0:T(8,128)(2,1)S(1)} %get-tuple-element.169.refs_0_, bf16[192,1408]{1,0:T(8,128)(2,1)S(1)} %collective-permute-done.11.refs_1_, bf16[96,1408]{1,0:T(8,128)(2,1)S(1)} %collective-permute-done.12.refs_2_, ...), custom_call_target="tpu_custom_call" | custom-call | flops 3300000000 | tf_op jit(solution)/shard_map/pallas_call | solution.py:91
  59.8 11.0 %shard_map.252 = (bf16[64,2048]{1,0:T(8,128)(2,1)}, bf16[64,2048]{1,0:T(8,128)(2,1)}, bf16[64,2048]{1,0:T(8,128)(2,1)}, bf16[64,2048]{1,0:T(8,128)(2,1)}, bf16[3...) custom-call(bf16[64,2304]{1,0:T(8,128)(2,1)S(1)} %copy-done.6, ...), custom_call_target="tpu_custom_call" | custom-call | flops 11000000512 | tf_op jit(solution)/shard_map/pallas_call | solution.py:91
  70.9 6.9 %shard_map.253 = (bf16[64,2176]{1,0:T(8,128)(2,1)}, bf16[64,2176]{1,0:T(8,128)(2,1)}, bf16[64,2176]{1,0:T(8,128)(2,1)}, bf16[64,2176]{1,0:T(8,128)(2,1)}, bf16[3...) custom-call(bf16[64,2304]{1,0:T(8,128)(2,1)S(1)} %copy-done.4, ...), custom_call_target="tpu_custom_call" | custom-call | flops 11000000512 | tf_op jit(solution)/shard_map/pallas_call | solution.py:91
  78.6 8.9 %collective-permute-done.22.refs_2_ = bf16[64,2176]{1,0:T(8,128)(2,1)S(1)} collective-permute-done((bf16[64,2176]{1,0:T(8,128)(2,1)}, bf16[64,2176]{1,0:T(8,128)(2,1)S(1)}, u32[]{:S(2)}, u32[]{:S(2)}) %collective-permute-start.22) | collective-permute-done | bytes 278560 | tf_op jit(solution)/shard_map/ppermute | solution.py:21
  87.4 6.4 %shard_map.259 = (bf16[2048,256]{1,0:T(8,128)(2,1)}, bf16[2048,256]{1,0:T(8,128)(2,1)}) custom-call(bf16[3,256,2304]{2,1,0:T(8,128)(2,1)S(1)} %get-tuple-element.209.refs_0_, bf16[3,256,2304]{2,1,0:T(8,128)(2,1)S(1)} %get-tuple-element.210.refs_1_, f32[1,2304]{1,0:T(1,128)S(1)} %reshape_reshape.3.refs_5_.refs_6_.refs_2_, ...), custom_call_target="tpu_custom_call" | custom-call | flops 8800000000 | tf_op jit(solution)/shard_map/pallas_call | solution.py:91
  96.8 6.4 %collective-permute-done.23.refs_3_ = bf16[64,2176]{1,0:T(8,128)(2,1)S(1)} collective-permute-done((bf16[64,2176]{1,0:T(8,128)(2,1)S(1)}, bf16[64,2176]{1,0:T(8,128)(2,1)S(1)}, u32[]{:S(2)}, u32[]{:S(2)}) %collective-permute-start.23) | collective-permute-done | bytes 278560 | tf_op jit(solution)/shard_map/ppermute | solution.py:21
  103.1 5.8 %shard_map.254 = (bf16[1024,1024]{1,0:T(8,128)(2,1)S(1)}, bf16[528,256]{1,0:T(8,128)(2,1)S(1)}, bf16[528,256]{1,0:T(8,128)(2,1)S(1)}, bf16[512,256]{1,0:T(8,128)(2,1)S(1)}, bf16[512,256]{1,0:T(8,128)(2,1)S(1)}) custom-call(bf16[64,2176]{1,0:T(8,128)(2,1)S(1)} %copy-done.5, bf16[64,2176]{1,0:T(8,128)(2,1)S(1)} %collective-permute-done.21.refs_1_, ...), custom_call_target="tpu_custom_call" | custom-call | flops 5500000256 | tf_op jit(solution)/shard_map/pallas_call | solution.py:91
  110.0 3.5 %shard_map.255 = (bf16[256,1024]{1,0:T(8,128)(2,1)}, bf16[256,1024]{1,0:T(8,128)(2,1)}) custom-call(bf16[1024,512]{1,0:T(8,128)(2,1)} %get-tuple-element.180.refs_0_, bf16[1024,1024]{1,0:T(8,128)(2,1)S(1)} %get-tuple-element.196.refs_1_), custom_call_target="tpu_custom_call" | custom-call | flops 3300000000 | tf_op jit(solution)/shard_map/pallas_call | solution.py:91
  115.4 7.0 %collective-permute-done.30.refs_1_ = bf16[512,256]{1,0:T(8,128)(2,1)S(1)} collective-permute-done((bf16[512,256]{1,0:T(8,128)(2,1)S(1)}, bf16[512,256]{1,0:T(8,128)(2,1)S(1)}, u32[]{:S(2)}, u32[]{:S(2)}) %collective-permute-start.30) | collective-permute-done | bytes 262176 | tf_op jit(solution)/shard_map/ppermute | solution.py:21
  128.5 4.7 %collective-permute-done.25.refs_1_ = bf16[128,1024]{1,0:T(8,128)(2,1)S(1)} collective-permute-done((bf16[128,1024]{1,0:T(8,128)(2,1)S(1)}, bf16[128,1024]{1,0:T(8,128)(2,1)S(1)}, u32[]{:S(2)}, u32[]{:S(2)}) %collective-permute-start.25) | collective-permute-done | bytes 262176 | tf_op jit(solution)/shard_map/ppermute | solution.py:21
  137.8 2.5 %collective-permute-start.35 = (bf16[400,256]{1,0:T(8,128)(2,1)S(1)}, bf16[400,256]{1,0:T(8,128)(2,1)S(1)}, u32[]{:S(2)}, u32[]{:S(2)}) collective-permute-start(bf16[400,256]{1,0:T(8,128)(2,1)S(1)} %get-tuple-element.225), channel_id=1, source_target_pairs={{0,16},{4,20},{8,24},{12,28},{16,0},{20,4},{24,8},{28,12},{1,17},{... | collective-permute-start | bytes 614408 | tf_op jit(solution)/shard_map/ppermute | solution.py:21
  145.1 3.4 %collective-permute-done.35.refs_1_ = bf16[400,256]{1,0:T(8,128)(2,1)S(1)} collective-permute-done((bf16[400,256]{1,0:T(8,128)(2,1)S(1)}, bf16[400,256]{1,0:T(8,128)(2,1)S(1)}, u32[]{:S(2)}, u32[]{:S(2)}) %collective-permute-start.35) | collective-permute-done | bytes 204832 | tf_op jit(solution)/shard_map/ppermute | solution.py:21
  150.6 4.5 %collective-permute-done.37 = bf16[128,256]{1,0:T(8,128)(2,1)S(1)} collective-permute-done((bf16[128,256]{1,0:T(8,128)(2,1)S(1)}, bf16[128,256]{1,0:T(8,128)(2,1)S(1)}, u32[]{:S(2)}, u32[]{:S(2)}) %collective-permute-start.37) | collective-permute-done | bytes 65568 | tf_op jit(solution)/shard_map/ppermute | solution.py:21
  155.9 2.9 %collective-permute-start.40 = (bf16[512,256]{1,0:T(8,128)(2,1)S(1)}, bf16[512,256]{1,0:T(8,128)(2,1)S(1)}, u32[]{:S(2)}, u32[]{:S(2)}) collective-permute-start(bf16[512,256]{1,0:T(8,128)(2,1)S(1)} %shard_map.267.refs_0_), channel_id=1, source_target_pairs={{0,16},{4,20},{8,24},{12,28},{16,0},{20,4},{24,8},{28,12},{1,17},{... | collective-permute-start | bytes 786440 | tf_op jit(solution)/shard_map/ppermute | solution.py:21
  160.5 4.0 %collective-permute-done.39 = bf16[256,256]{1,0:T(8,128)(2,1)S(1)} collective-permute-done((bf16[256,256]{1,0:T(8,128)(2,1)S(1)}, bf16[256,256]{1,0:T(8,128)(2,1)S(1)}, u32[]{:S(2)}, u32[]{:S(2)}) %collective-permute-start.39) | collective-permute-done | bytes 131104 | tf_op jit(solution)/shard_map/ppermute | solution.py:21
  164.5 4.4 %collective-permute-done.40.refs_1_ = bf16[512,256]{1,0:T(8,128)(2,1)S(1)} collective-permute-done((bf16[512,256]{1,0:T(8,128)(2,1)S(1)}, bf16[512,256]{1,0:T(8,128)(2,1)S(1)}, u32[]{:S(2)}, u32[]{:S(2)}) %collective-permute-start.40) | collective-permute-done | bytes 262176 | tf_op jit(solution)/shard_map/ppermute | solution.py:21
  175.7 4.4 %collective-permute-done.42.refs_3_ = bf16[1024,256]{1,0:T(8,128)(2,1)S(1)} collective-permute-done((bf16[1024,256]{1,0:T(8,128)(2,1)S(1)}, bf16[1024,256]{1,0:T(8,128)(2,1)S(1)}, u32[]{:S(2)}, u32[]{:S(2)}) %collective-permute-start.42) | collective-permute-done | bytes 524320 | tf_op jit(solution)/shard_map/ppermute | solution.py:21
  180.1 5.5 %shard_map.269 = (f32[16,64,512]{2,1,0:T(8,128)}, f32[1,512]{1,0:T(1,128)}, f32[3,3,64,256]{3,2,1,0:T(8,128)}, f32[3,64]{1,0:T(4,128)}, f32[3,64]{1,0:T(4,128)},...) custom-call(bf16[512,256]{1,0:T(8,128)(2,1)S(1)} %constant_dynamic-u, ...), custom_call_target="tpu_custom_call" | custom-call | flops 5500000256 | tf_op jit(solution)/shard_map/pallas_call | solution.py:91
  (139 shorter events, 56.8 us)
Async XLA Ops:
  1.5 13.6 %collective-permute-start.1 = (bf16[192,128]{1,0:T(8,128)(2,1)S(1)}, bf16[192,128]{1,0:T(8,128)(2,1)S(1)}, u32[]{:S(2)}, u32[]{:S(2)}) collective-permute-start(bf16[192,128]{1,0:T(8,128)(2,1)S(1)} %get-tuple-element.133), channel_id=1, source_target_pairs={{4,0},{8,4},{12,8},{16,12},{20,16},{24,20},{28,24},{5,1},{9,5},{13... | collective-permute-start | bytes 147464 | tf_op jit(solution)/shard_map/ppermute | solution.py:850
  2.8 12.3 %collective-permute-start = (bf16[192,128]{1,0:T(8,128)(2,1)S(1)}, bf16[192,128]{1,0:T(8,128)(2,1)S(1)}, u32[]{:S(2)}, u32[]{:S(2)}) collective-permute-start(bf16[192,128]{1,0:T(8,128)(2,1)S(1)} %get-tuple-element.132), channel_id=1, source_target_pairs={{0,4},{4,8},{8,12},{12,16},{16,20},{20,24},{24,28},{1,5},{5,9},{9,... | collective-permute-start | bytes 147464 | tf_op jit(solution)/shard_map/ppermute | solution.py:849
  13.5 11.1 %collective-permute-start.6 = (bf16[128,1024]{1,0:T(8,128)(2,1)S(1)}, bf16[128,1024]{1,0:T(8,128)(2,1)S(1)}, u32[]{:S(2)}, u32[]{:S(2)}) collective-permute-start(bf16[128,1024]{1,0:T(8,128)(2,1)S(1)} %copy-done), channel_id=1, source_target_pairs={{0,2},{1,3},{2,0},{3,1},{4,6},{5,7},{6,4},{7,5},{8,10},{9,11},{10,... | collective-permute-start | bytes 786440 | tf_op jit(solution)/shard_map/ppermute | solution.py:21
  24.5 9.5 %collective-permute-start.5 = (bf16[128,1024]{1,0:T(8,128)(2,1)S(1)}, bf16[128,1024]{1,0:T(8,128)(2,1)S(1)}, u32[]{:S(2)}, u32[]{:S(2)}) collective-permute-start(bf16[128,1024]{1,0:T(8,128)(2,1)S(1)} %copy-done), channel_id=1, source_target_pairs={{0,1},{1,0},{2,3},{3,2},{4,5},{5,4},{6,7},{7,6},{8,9},{9,8},{10,11... | collective-permute-start | bytes 786440 | tf_op jit(solution)/shard_map/ppermute | solution.py:21
  26.5 17.2 %collective-permute-start.11 = (bf16[192,1408]{1,0:T(8,128)(2,1)S(1)}, bf16[192,1408]{1,0:T(8,128)(2,1)S(1)}, u32[]{:S(2)}, u32[]{:S(2)}) collective-permute-start(bf16[192,1408]{1,0:T(8,128)(2,1)S(1)} %get-tuple-element.169.refs_0_), channel_id=1, source_target_pairs={{0,1},{1,0},{2,3},{3,2},{4,5},{5,4},{6,7},{7,6},{8,9},{9,8},{10,11... | collective-permute-start | bytes 1622024 | tf_op jit(solution)/shard_map/ppermute | solution.py:21
  31.6 12.1 %collective-permute-start.13 = (bf16[96,1408]{1,0:T(8,128)(2,1)S(1)}, bf16[96,1408]{1,0:T(8,128)(2,1)S(1)}, u32[]{:S(2)}, u32[]{:S(2)}) collective-permute-start(bf16[96,1408]{1,0:T(8,128)(2,1)S(1)} %collective-permute-done.12.refs_2_), channel_id=1, source_target_pairs={{0,4},{4,0},{8,12},{12,8},{16,20},{20,16},{24,28},{28,24},{1,5},{5... | collective-permute-start | bytes 811016 | tf_op jit(solution)/shard_map/ppermute | solution.py:21
  41.5 10.1 %collective-permute-start.16 = (bf16[64,2304]{1,0:T(8,128)(2,1)}, bf16[64,2304]{1,0:T(8,128)(2,1)S(1)}, u32[]{:S(2)}, u32[]{:S(2)}) collective-permute-start(bf16[64,2304]{1,0:T(8,128)(2,1)} %get-tuple-element.162), channel_id=1, source_target_pairs={{0,2},{1,3},{2,0},{3,1},{4,6},{5,7},{6,4},{7,5},{8,10},{9,11},{10,... | collective-permute-start | bytes 884744 | tf_op jit(solution)/shard_map/ppermute | solution.py:21
  42.1 9.5 %collective-permute-start.10 = (bf16[64,2304]{1,0:T(8,128)(2,1)}, bf16[64,2304]{1,0:T(8,128)(2,1)S(1)}, u32[]{:S(2)}, u32[]{:S(2)}) collective-permute-start(bf16[64,2304]{1,0:T(8,128)(2,1)} %get-tuple-element.159), channel_id=1, source_target_pairs={{0,1},{1,0},{2,3},{3,2},{4,5},{5,4},{6,7},{7,6},{8,9},{9,8},{10,11... | collective-permute-start | bytes 884744 | tf_op jit(solution)/shard_map/ppermute | solution.py:21
  42.1 10.9 %collective-permute-start.17 = (bf16[64,2304]{1,0:T(8,128)(2,1)}, bf16[64,2304]{1,0:T(8,128)(2,1)S(1)}, u32[]{:S(2)}, u32[]{:S(2)}) collective-permute-start(bf16[64,2304]{1,0:T(8,128)(2,1)} %get-tuple-element.164), channel_id=1, source_target_pairs={{0,3},{1,2},{2,1},{3,0},{4,7},{5,6},{6,5},{7,4},{8,11},{9,10},{10,... | collective-permute-start | bytes 884744 | tf_op jit(solution)/shard_map/ppermute | solution.py:21
  53.0 17.8 %collective-permute-start.18 = (bf16[64,2304]{1,0:T(8,128)(2,1)}, bf16[64,2304]{1,0:T(8,128)(2,1)S(1)}, u32[]{:S(2)}, u32[]{:S(2)}) collective-permute-start(bf16[64,2304]{1,0:T(8,128)(2,1)} %get-tuple-element.182), channel_id=1, source_target_pairs={{0,1},{1,0},{2,3},{3,2},{4,5},{5,4},{6,7},{7,6},{8,9},{9,8},{10,11... | collective-permute-start | bytes 884744 | tf_op jit(solution)/shard_map/ppermute | solution.py:21
  54.6 16.2 %collective-permute-start.19 = (bf16[64,2304]{1,0:T(8,128)(2,1)}, bf16[64,2304]{1,0:T(8,128)(2,1)S(1)}, u32[]{:S(2)}, u32[]{:S(2)}) collective-permute-start(bf16[64,2304]{1,0:T(8,128)(2,1)} %get-tuple-element.183), channel_id=1, source_target_pairs={{0,2},{1,3},{2,0},{3,1},{4,6},{5,7},{6,4},{7,5},{8,10},{9,11},{10,... | collective-permute-start | bytes 884744 | tf_op jit(solution)/shard_map/ppermute | solution.py:21
  55.2 15.7 %collective-permute-start.20 = (bf16[64,2304]{1,0:T(8,128)(2,1)}, bf16[64,2304]{1,0:T(8,128)(2,1)S(1)}, u32[]{:S(2)}, u32[]{:S(2)}) collective-permute-start(bf16[64,2304]{1,0:T(8,128)(2,1)} %get-tuple-element.184), channel_id=1, source_target_pairs={{0,3},{1,2},{2,1},{3,0},{4,7},{5,6},{6,5},{7,4},{8,11},{9,10},{10,... | collective-permute-start | bytes 884744 | tf_op jit(solution)/shard_map/ppermute | solution.py:21
  77.8 9.6 %collective-permute-start.22 = (bf16[64,2176]{1,0:T(8,128)(2,1)}, bf16[64,2176]{1,0:T(8,128)(2,1)S(1)}, u32[]{:S(2)}, u32[]{:S(2)}) collective-permute-start(bf16[64,2176]{1,0:T(8,128)(2,1)} %get-tuple-element.192), channel_id=1, source_target_pairs={{0,2},{1,3},{2,0},{3,1},{4,6},{5,7},{6,4},{7,5},{8,10},{9,11},{10,... | collective-permute-start | bytes 835592 | tf_op jit(solution)/shard_map/ppermute | solution.py:21
  93.9 15.1 %collective-permute-start.31 = (bf16[2048,256]{1,0:T(8,128)(2,1)}, bf16[2048,256]{1,0:T(8,128)(2,1)S(1)}, u32[]{:S(2)}, u32[]{:S(2)}) collective-permute-start(bf16[2048,256]{1,0:T(8,128)(2,1)} %get-tuple-element.215), channel_id=1, source_target_pairs={{0,1},{1,0},{2,3},{3,2},{4,5},{5,4},{6,7},{7,6},{8,9},{9,8},{10,11... | collective-permute-start | bytes 3145736 | tf_op jit(solution)/shard_map/ppermute | solution.py:21
  109.4 14.0 %collective-permute-start.32 = (bf16[1024,256]{1,0:T(8,128)(2,1)S(1)}, bf16[1024,256]{1,0:T(8,128)(2,1)S(1)}, u32[]{:S(2)}, u32[]{:S(2)}) collective-permute-start(bf16[1024,256]{1,0:T(8,128)(2,1)S(1)} %get-tuple-element.217), channel_id=1, source_target_pairs={{0,2},{1,3},{2,0},{3,1},{4,6},{5,7},{6,4},{7,5},{8,10},{9,11},{10,... | collective-permute-start | bytes 1572872 | tf_op jit(solution)/shard_map/ppermute | solution.py:21
  113.6 12.1 %collective-permute-start.24 = (bf16[256,1024]{1,0:T(8,128)(2,1)}, bf16[256,1024]{1,0:T(8,128)(2,1)S(1)}, u32[]{:S(2)}, u32[]{:S(2)}) collective-permute-start(bf16[256,1024]{1,0:T(8,128)(2,1)} %get-tuple-element.198), channel_id=1, source_target_pairs={{0,1},{1,0},{2,3},{3,2},{4,5},{5,4},{6,7},{7,6},{8,9},{9,8},{10,11... | collective-permute-start | bytes 1572872 | tf_op jit(solution)/shard_map/ppermute | solution.py:21
  124.0 13.3 %collective-permute-start.33 = (bf16[784,256]{1,0:T(8,128)(2,1)S(1)}, bf16[784,256]{1,0:T(8,128)(2,1)S(1)}, u32[]{:S(2)}, u32[]{:S(2)}) collective-permute-start(bf16[784,256]{1,0:T(8,128)(2,1)S(1)} %get-tuple-element.219), channel_id=1, source_target_pairs={{0,8},{4,12},{8,0},{12,4},{16,24},{20,28},{24,16},{28,20},{1,9},{5... | collective-permute-start | bytes 1204232 | tf_op jit(solution)/shard_map/ppermute | solution.py:21
  126.7 9.7 %collective-permute-start.34 = (bf16[256,256]{1,0:T(8,128)(2,1)S(1)}, bf16[256,256]{1,0:T(8,128)(2,1)S(1)}, u32[]{:S(2)}, u32[]{:S(2)}) collective-permute-start(bf16[256,256]{1,0:T(8,128)(2,1)S(1)} %get-tuple-element.222), channel_id=1, source_target_pairs={{0,16},{4,20},{8,24},{12,28},{16,0},{20,4},{24,8},{28,12},{1,17},{... | collective-permute-start | bytes 393224 | tf_op jit(solution)/shard_map/ppermute | solution.py:21
  133.2 35.9 %collective-permute-start.26 = (bf16[64,2048]{1,0:T(8,128)(2,1)S(1)}, bf16[64,2048]{1,0:T(8,128)(2,1)S(1)}, u32[]{:S(2)}, u32[]{:S(2)}) collective-permute-start(bf16[64,2048]{1,0:T(8,128)(2,1)S(1)} %copy-done.12), channel_id=1, source_target_pairs={{0,1},{1,0},{2,3},{3,2},{4,5},{5,4},{6,7},{7,6},{8,9},{9,8},{10,11... | collective-permute-start | bytes 786440 | tf_op jit(solution)/shard_map/ppermute | solution.py:21
  133.2 36.9 %collective-permute-start.27 = (bf16[64,2048]{1,0:T(8,128)(2,1)S(1)}, bf16[64,2048]{1,0:T(8,128)(2,1)S(1)}, u32[]{:S(2)}, u32[]{:S(2)}) collective-permute-start(bf16[64,2048]{1,0:T(8,128)(2,1)S(1)} %copy-done.11), channel_id=1, source_target_pairs={{0,2},{1,3},{2,0},{3,1},{4,6},{5,7},{6,4},{7,5},{8,10},{9,11},{10,... | collective-permute-start | bytes 786440 | tf_op jit(solution)/shard_map/ppermute | solution.py:21
  134.2 35.8 %collective-permute-start.28 = (bf16[64,2048]{1,0:T(8,128)(2,1)S(1)}, bf16[64,2048]{1,0:T(8,128)(2,1)S(1)}, u32[]{:S(2)}, u32[]{:S(2)}) collective-permute-start(bf16[64,2048]{1,0:T(8,128)(2,1)S(1)} %copy-done.10), channel_id=1, source_target_pairs={{0,3},{1,2},{2,1},{3,0},{4,7},{5,6},{6,5},{7,4},{8,11},{9,10},{10,... | collective-permute-start | bytes 786440 | tf_op jit(solution)/shard_map/ppermute | solution.py:21
  137.8 10.7 %collective-permute-start.35 = (bf16[400,256]{1,0:T(8,128)(2,1)S(1)}, bf16[400,256]{1,0:T(8,128)(2,1)S(1)}, u32[]{:S(2)}, u32[]{:S(2)}) collective-permute-start(bf16[400,256]{1,0:T(8,128)(2,1)S(1)} %get-tuple-element.225), channel_id=1, source_target_pairs={{0,16},{4,20},{8,24},{12,28},{16,0},{20,4},{24,8},{28,12},{1,17},{... | collective-permute-start | bytes 614408 | tf_op jit(solution)/shard_map/ppermute | solution.py:21
  155.9 13.0 %collective-permute-start.40 = (bf16[512,256]{1,0:T(8,128)(2,1)S(1)}, bf16[512,256]{1,0:T(8,128)(2,1)S(1)}, u32[]{:S(2)}, u32[]{:S(2)}) collective-permute-start(bf16[512,256]{1,0:T(8,128)(2,1)S(1)} %shard_map.267.refs_0_), channel_id=1, source_target_pairs={{0,16},{4,20},{8,24},{12,28},{16,0},{20,4},{24,8},{28,12},{1,17},{... | collective-permute-start | bytes 786440 | tf_op jit(solution)/shard_map/ppermute | solution.py:21
  169.0 11.1 %collective-permute-start.42 = (bf16[1024,256]{1,0:T(8,128)(2,1)S(1)}, bf16[1024,256]{1,0:T(8,128)(2,1)S(1)}, u32[]{:S(2)}, u32[]{:S(2)}) collective-permute-start(bf16[1024,256]{1,0:T(8,128)(2,1)S(1)} %shard_map.268.refs_2_), channel_id=1, source_target_pairs={{0,8},{4,12},{8,0},{12,4},{16,24},{20,28},{24,16},{28,20},{1,9},{5... | collective-permute-start | bytes 1572872 | tf_op jit(solution)/shard_map/ppermute | solution.py:21
  (34 other events, 247.3 us)
